TPU v7x, 256 devices: a whole 4x4x8 slice. The times are simulated.
256 devices in a mesh: section: 4 (over y), dp: 16 (over z, x_lo), tensor: 4 (over x_hi, core).
Axes of the slice: x: 4 (x_hi: 2, x_lo: 2; x = x_hi * 2 + x_lo), y: 4, z: 8, core: 2. Of those that a mesh axis runs over, the one named last changes fastest.
Arguments:
- hidden_in: bfloat16 [16, 2, 64, 4096], P('dp', None, None, 'tensor'), may hold values from -6 to 6
- teacher: bfloat16 [16, 2, 64, 4096], P('dp', None, None, 'tensor'), may hold values from -6 to 6
- segment_ids: int32 [16, 2, 64], P('dp'), may hold values from 0 to 3, never falling along the last dimension, each value on 1 to 32 neighbouring positions
- w_query: bfloat16 [4, 4096, 4096], P('section', None, 'tensor'), may hold values from -0.09375 to 0.09375
- w_keyval: bfloat16 [4, 4096, 1024], P('section', None, 'tensor'), may hold values from -0.09375 to 0.09375
- norm_gain: bfloat16 [4, 4096], P('section', 'tensor'), may hold values from 0.5 to 1.5
Outputs:
- grad_query: float32 [4, 4096, 4096], P('section', 'dp', 'tensor')
- grad_keyval: float32 [4, 4096, 1024], P('section', 'dp', 'tensor')
- grad_gains: float32 [4, 4096], P('section', ('tensor', 'dp'))
- layer_input_grads: bfloat16 [4, 16, 2, 64, 4096], P('section', 'dp', None, None, 'tensor')
Inputs may be any that keep to these rules, and one draw needn't show every extreme that they name: `segment_ids`: along each sequence the ids never fall.
All inputs are finite; a program needn't handle non-finite values.
Results may differ from a plain program's by a relative error of at most 0.03.
Values may be sent and summed in bfloat16 or wider, within the bound.
A program may use at most 128 MiB of HBM per device.

v0:
```python
import math

import jax
import jax.numpy as jnp
from jax import lax
from jax.sharding import PartitionSpec as P

D = 4096
HD = 128


EPSILON = 1e-05


def passed_along(array, axis, by):
    length = lax.axis_size(axis)
    return lax.ppermute(array, axis, [(i, (i + by) % length) for i in range(length)])


def attend_forward(queries, keyvals, segments, head_size):
    length = queries.shape[0]
    shared_heads = keyvals.shape[1] // (2 * head_size)
    group_size = queries.shape[1] // head_size // shared_heads
    query_heads = queries.reshape(length, shared_heads, group_size, head_size)
    key_value = keyvals.reshape(length, shared_heads, 2, head_size)
    score_scale = 1.0 / math.sqrt(head_size)
    scores = (
        jnp.einsum(
            "qhgd,khd->hgqk", query_heads, key_value[:, :, 0], preferred_element_type=jnp.float32
        )
        * score_scale
    )
    query_pos = lax.broadcasted_iota(jnp.int32, (length, length), 0)
    key_pos = lax.broadcasted_iota(jnp.int32, (length, length), 1)
    allowed = (segments[:, None] == segments[None, :]) & (query_pos >= key_pos)
    exponent = jnp.exp(jnp.where(allowed, scores, -jnp.inf))
    probabilities = exponent / jnp.sum(exponent, axis=-1, keepdims=True)
    weights = probabilities.astype(jnp.bfloat16)
    heads_out = jnp.einsum(
        "hgqk,khd->qhgd", weights, key_value[:, :, 1], preferred_element_type=jnp.float32
    )
    return (heads_out.reshape(length, -1).astype(jnp.bfloat16), probabilities, weights)


def attend_backward(grad_out, queries, keyvals, probabilities, weights, head_size):
    length = queries.shape[0]
    shared_heads = keyvals.shape[1] // (2 * head_size)
    group_size = queries.shape[1] // head_size // shared_heads
    query_heads = queries.reshape(length, shared_heads, group_size, head_size)
    key_value = keyvals.reshape(length, shared_heads, 2, head_size)
    grad_heads = grad_out.reshape(length, shared_heads, group_size, head_size)
    score_scale = 1.0 / math.sqrt(head_size)
    grad_probs = jnp.einsum(
        "qhgd,khd->hgqk", grad_heads, key_value[:, :, 1], preferred_element_type=jnp.float32
    )
    centered = grad_probs - jnp.sum(grad_probs * probabilities, axis=-1, keepdims=True)
    grad_scores = (probabilities * centered).astype(jnp.bfloat16)
    grad_query = (
        jnp.einsum(
            "hgqk,khd->qhgd", grad_scores, key_value[:, :, 0], preferred_element_type=jnp.float32
        )
        * score_scale
    ).astype(jnp.bfloat16)
    grad_key = (
        jnp.einsum("hgqk,qhgd->khd", grad_scores, query_heads, preferred_element_type=jnp.float32)
        * score_scale
    ).astype(jnp.bfloat16)
    grad_value = jnp.einsum(
        "hgqk,qhgd->khd", weights, grad_heads, preferred_element_type=jnp.float32
    ).astype(jnp.bfloat16)
    grad_pairs = jnp.stack([grad_key, grad_value], axis=2)
    return (grad_query.reshape(length, -1), grad_pairs.reshape(length, -1))


def keep_slot(store, value, target_slot, active):
    updated = lax.dynamic_update_index_in_dim(store, value, target_slot, 0)
    return jnp.where(active, updated, store)


def pick_slot(store, target_slot):
    return lax.dynamic_index_in_dim(store, target_slot, 0, keepdims=False)


def body(hidden_in, teacher, segment_ids, w_query, w_keyval, norm_gain):
    sections = lax.axis_size("section")
    section_id = lax.axis_index("section")
    micro_count = hidden_in.shape[1]
    length = hidden_in.shape[2]
    local_width = hidden_in.shape[3]
    query_proj = w_query[0]
    keyval_proj = w_keyval[0]
    gains = norm_gain[0]
    gains_wide = gains.astype(jnp.float32)
    query_cols = query_proj.shape[1]
    keyval_cols = keyval_proj.shape[1]
    timesteps = micro_count + sections - 1

    def local_forward(operands):
        gathered, segments = operands
        queries = jnp.dot(gathered, query_proj, preferred_element_type=jnp.float32).astype(
            jnp.bfloat16
        )
        keyvals = jnp.dot(gathered, keyval_proj, preferred_element_type=jnp.float32).astype(
            jnp.bfloat16
        )
        heads_out, unused_probs, unused_weights = attend_forward(queries, keyvals, segments, HD)
        return (heads_out, queries, keyvals)

    def skip_forward(operands):
        return (
            jnp.zeros((length, query_cols), jnp.bfloat16),
            jnp.zeros((length, query_cols), jnp.bfloat16),
            jnp.zeros((length, keyval_cols), jnp.bfloat16),
        )

    inbound = jnp.zeros((length, local_width), jnp.bfloat16)
    kept_rows = jnp.zeros((micro_count, length, local_width), jnp.bfloat16)
    kept_wide = jnp.zeros((micro_count, length, D), jnp.bfloat16)
    kept_query = jnp.zeros((micro_count, length, query_cols), jnp.bfloat16)
    kept_keyval = jnp.zeros((micro_count, length, keyval_cols), jnp.bfloat16)
    kept_inverse = jnp.zeros((micro_count, length), jnp.float32)
    finals = jnp.zeros((micro_count, length, local_width), jnp.bfloat16)
    for timestep in range(timesteps):
        if timestep < micro_count:
            current = jnp.where(section_id == 0, hidden_in[0, timestep], inbound)
        else:
            current = inbound
        position = timestep - section_id
        active = (position >= 0) & (position < micro_count)
        target_slot = jnp.clip(position, 0, micro_count - 1)
        segments = pick_slot(segment_ids[0], target_slot)
        normalize_widened = current.astype(jnp.float32)
        squares = lax.psum(jnp.sum(normalize_widened * normalize_widened, axis=1), "tensor")
        inverse = lax.rsqrt(squares / D + EPSILON)
        normed = (normalize_widened * inverse[:, None] * gains_wide).astype(jnp.bfloat16)
        normalize_gathered = lax.all_gather(normed, "tensor", axis=1, tiled=True)
        gathered, inverse = (normalize_gathered, inverse)
        heads_out, queries, keyvals = lax.cond(
            active, local_forward, skip_forward, (gathered, segments)
        )
        output = (current.astype(jnp.float32) + heads_out.astype(jnp.float32)).astype(jnp.bfloat16)
        kept_rows = keep_slot(kept_rows, current, target_slot, active)
        kept_wide = keep_slot(kept_wide, gathered, target_slot, active)
        kept_query = keep_slot(kept_query, queries, target_slot, active)
        kept_keyval = keep_slot(kept_keyval, keyvals, target_slot, active)
        kept_inverse = keep_slot(kept_inverse, inverse, target_slot, active)
        inbound = passed_along(output, "section", 1)
        arrived = timestep - (sections - 1)
        if arrived >= 0:
            finals = finals.at[arrived].set(inbound)
    loss_grads = (finals.astype(jnp.float32) - teacher[0].astype(jnp.float32)).astype(jnp.bfloat16)

    def local_backward(operands):
        incoming, queries, keyvals, segments = operands
        unused_out, probabilities, weights = attend_forward(queries, keyvals, segments, HD)
        grad_query, grad_keyval = attend_backward(
            incoming, queries, keyvals, probabilities, weights, HD
        )
        partial_value = jnp.einsum(
            "lc,dc->ld", grad_query, query_proj, preferred_element_type=jnp.float32
        )
        partial_value = partial_value + jnp.einsum(
            "lc,dc->ld", grad_keyval, keyval_proj, preferred_element_type=jnp.float32
        )
        return (grad_query, grad_keyval, partial_value)

    def skip_backward(operands):
        return (
            jnp.zeros((length, query_cols), jnp.bfloat16),
            jnp.zeros((length, keyval_cols), jnp.bfloat16),
            jnp.zeros((length, D), jnp.float32),
        )

    sum_gains = jnp.zeros((local_width,), jnp.float32)
    saved_grad_query = jnp.zeros((micro_count, length, query_cols), jnp.bfloat16)
    saved_grad_keyval = jnp.zeros((micro_count, length, keyval_cols), jnp.bfloat16)
    layer_grads = jnp.zeros((micro_count, length, local_width), jnp.bfloat16)
    previous = jnp.zeros((length, local_width), jnp.bfloat16)
    for timestep in range(timesteps):
        if timestep < micro_count:
            outgoing = jnp.where(section_id == 0, loss_grads[timestep], previous)
        else:
            outgoing = previous
        incoming = passed_along(outgoing, "section", -1)
        position = timestep - (sections - 1 - section_id)
        active = (position >= 0) & (position < micro_count)
        target_slot = jnp.clip(position, 0, micro_count - 1)
        segments = pick_slot(segment_ids[0], target_slot)
        rows_kept = pick_slot(kept_rows, target_slot)
        inverse_kept = pick_slot(kept_inverse, target_slot)
        operands = (
            incoming,
            pick_slot(kept_query, target_slot),
            pick_slot(kept_keyval, target_slot),
            segments,
        )
        results = lax.cond(active, local_backward, skip_backward, operands)
        grad_normed = lax.psum_scatter(
            results[2].astype(jnp.bfloat16), "tensor", scatter_dimension=1, tiled=True
        ).astype(jnp.float32)
        widened = rows_kept.astype(jnp.float32)
        scaled = grad_normed * gains_wide
        row_dots = lax.psum(jnp.sum(scaled * widened, axis=1), "tensor")
        grad_rows = (
            incoming.astype(jnp.float32)
            + inverse_kept[:, None] * scaled
            - widened * (inverse_kept**3 * row_dots / D)[:, None]
        )
        grad_block = grad_rows.astype(jnp.bfloat16)
        sum_gains = sum_gains + jnp.where(
            active, jnp.sum(grad_normed * widened * inverse_kept[:, None], axis=0), 0.0
        )
        saved_grad_query = keep_slot(saved_grad_query, results[0], target_slot, active)
        saved_grad_keyval = keep_slot(saved_grad_keyval, results[1], target_slot, active)
        layer_grads = keep_slot(layer_grads, grad_block, target_slot, active)
        previous = grad_block
    rows_local = micro_count * length
    flat_wide = kept_wide.reshape(rows_local, D)
    flat_query = saved_grad_query.reshape(rows_local, query_cols)
    flat_keyval = saved_grad_keyval.reshape(rows_local, keyval_cols)
    term_query = jnp.dot(flat_wide.T, flat_query, preferred_element_type=jnp.float32)
    term_keyval = jnp.dot(flat_wide.T, flat_keyval, preferred_element_type=jnp.float32)
    grad_query, grad_keyval, grad_gains = (
        lax.psum_scatter(
            term_query.astype(jnp.bfloat16), "dp", scatter_dimension=0, tiled=True
        ).astype(jnp.float32),
        lax.psum_scatter(
            term_keyval.astype(jnp.bfloat16), "dp", scatter_dimension=0, tiled=True
        ).astype(jnp.float32),
        lax.psum_scatter(
            sum_gains.astype(jnp.bfloat16), "dp", scatter_dimension=0, tiled=True
        ).astype(jnp.float32),
    )
    return (grad_query[None], grad_keyval[None], grad_gains[None], layer_grads[None, None])


def solution(mesh):
    in_specs = (
        P("dp", None, None, "tensor"),
        P("dp", None, None, "tensor"),
        P("dp", None, None),
        P("section", None, "tensor"),
        P("section", None, "tensor"),
        P("section", "tensor"),
    )
    out_specs = (
        P("section", "dp", "tensor"),
        P("section", "dp", "tensor"),
        P("section", ("tensor", "dp")),
        P("section", "dp", None, None, "tensor"),
    )
    return jax.shard_map(body, mesh=mesh, in_specs=in_specs, out_specs=out_specs, check_vma=False)
```

profile of v0, /device:TPU:2, one launch (start us, length us, event | category | flops | bytes accessed | tf_op | source)
XLA Modules:
  0.0 775.7 jit_solution(777188976630663114)
XLA Ops:
  8.3 9.0 %psum.70 = f32[64]{0:T(128)S(1)} all-reduce(f32[64]{0:T(128)S(1)} %fusion.217), channel_id=1, replica_groups=mesh['section'=4,'dp'=16,'tensor'=4] {'tensor'}, use_global_device_ids=true, to_apply=%region_1.2 | all-reduce | flops 64 | bytes 512 | tf_op jit(solution)/shard_map/psum | solution.py:133
  19.0 8.5 %all_gather.15 = bf16[64,4096]{1,0:T(8,128)(2,1)} all-gather(bf16[64,1024]{1,0:T(8,128)(2,1)S(1)} %fusion.219), channel_id=1, replica_groups=mesh['section'=4,'dp'=16,'tensor'=4] {'tensor'}, dimensions={1}, use_global_device_ids=true | all-gather | bytes 655360 | tf_op jit(solution)/shard_map/all_gather | solution.py:136
  27.5 11.9 %conditional.10 = (bf16[64,1024]{1,0:T(8,128)(2,1)}, bf16[64,256]{1,0:T(8,128)(2,1)}, f32[64,1024]{1,0:T(8,128)S(1)}) conditional(s32[]{:T(128)} %convert_element_type.607, () %tuple.172, (bf16[64,4096]{1,0:T(8,128)(2,1)}, bf16[4096,1024]{1,0:T(8,128)(2,1)}, bf16[4096,256]{1,0:T(8,128)(2,1)}, s32[1,2,64]{2,1,0:T(2,128)}, s32[]{:T(128)}) %tuple.277), branch_computations={%region_2.3_spmd, %region_3.5_spmd} | conditional | flops 688254464 | bytes 13579036 | solution.py:138
  28.3 2.8 convolution_convert_fusion.2
  31.1 5.8 convolution_convert_fusion
  40.5 1.6 bitcast_dynamic-update-slice_fusion.3
  42.8 3.7 collective-permute-done
  46.7 7.7 psum.71
  54.5 8.5 %all_gather.16 = bf16[64,4096]{1,0:T(8,128)(2,1)} all-gather(bf16[64,1024]{1,0:T(8,128)(2,1)S(1)} %fusion.203), channel_id=1, replica_groups=mesh['section'=4,'dp'=16,'tensor'=4] {'tensor'}, dimensions={1}, use_global_device_ids=true | all-gather | bytes 655360 | tf_op jit(solution)/shard_map/all_gather | solution.py:136
  63.0 11.9 %conditional.11 = (f32[64,1024]{1,0:T(8,128)S(1)}, bf16[1,64,1024]{2,1,0:T(8,128)(2,1)}, bf16[1,64,256]{2,1,0:T(8,128)(2,1)}) conditional(s32[]{:T(128)} %convert_element_type.611, () %tuple.174, (bf16[64,4096]{1,0:T(8,128)(2,1)}, bf16[4096,256]{1,0:T(8,128)(2,1)}, s32[1,2,64]{2,1,0:T(2,128)}, s32[]{:T(128)}, bf16[4096,1024]{1,0:T(8,128)(2,1)}) %tuple.278), branch_computations={%region_7.8_spmd, %region_8.10_spmd} | conditional | flops 688254464 | bytes 13579036 | solution.py:138
  63.8 2.9 convolution_convert_fusion.5
  66.6 5.8 convolution_convert_fusion.3
  75.0 1.7 select_dynamic-update-slice_fusion.9
  77.5 4.5 collective-permute-done.1
  82.1 8.5 %psum.72 = f32[64]{0:T(128)S(1)} all-reduce(f32[64]{0:T(128)S(1)} %fusion.205), channel_id=1, replica_groups=mesh['section'=4,'dp'=16,'tensor'=4] {'tensor'}, use_global_device_ids=true, to_apply=%region_11.12 | all-reduce | flops 64 | bytes 512 | tf_op jit(solution)/shard_map/psum | solution.py:133
  90.7 8.5 %all_gather.17 = bf16[64,4096]{1,0:T(8,128)(2,1)} all-gather(bf16[64,1024]{1,0:T(8,128)(2,1)S(1)} %fusion.207), channel_id=1, replica_groups=mesh['section'=4,'dp'=16,'tensor'=4] {'tensor'}, dimensions={1}, use_global_device_ids=true | all-gather | bytes 655360 | tf_op jit(solution)/shard_map/all_gather | solution.py:136
  100.5 10.0 %collective-permute-start.2 = (bf16[64,1024]{1,0:T(8,128)(2,1)S(1)}, bf16[64,1024]{1,0:T(8,128)(2,1)S(1)}, u32[]{:S(2)}, u32[]{:S(2)}) collective-permute-start(bf16[64,1024]{1,0:T(8,128)(2,1)S(1)} %fusion.208), channel_id=1, source_target_pairs={{0,64},{64,128},{128,192},{192,0},{1,65},{65,129},{129,193},{193,1... | collective-permute-start | bytes 393224 | tf_op jit(solution)/shard_map/ppermute | solution.py:17
  110.5 1.6 select_dynamic-update-slice_fusion.8
  112.1 1.6 collective-permute-done.2
  113.8 8.0 %psum.73 = f32[64]{0:T(128)S(1)} all-reduce(f32[64]{0:T(128)S(1)} %fusion.209), channel_id=1, replica_groups=mesh['section'=4,'dp'=16,'tensor'=4] {'tensor'}, use_global_device_ids=true, to_apply=%region_16.17 | all-reduce | flops 64 | bytes 512 | tf_op jit(solution)/shard_map/psum | solution.py:133
  122.0 8.5 %all_gather.18 = bf16[64,4096]{1,0:T(8,128)(2,1)} all-gather(bf16[64,1024]{1,0:T(8,128)(2,1)S(1)} %fusion.211), channel_id=1, replica_groups=mesh['section'=4,'dp'=16,'tensor'=4] {'tensor'}, dimensions={1}, use_global_device_ids=true | all-gather | bytes 655360 | tf_op jit(solution)/shard_map/all_gather | solution.py:136
  132.0 2.6 collective-permute-start.3
  134.6 1.6 select_dynamic-update-slice_fusion.7
  136.2 11.7 %collective-permute-done.3 = bf16[64,1024]{1,0:T(8,128)(2,1)S(1)} collective-permute-done((bf16[64,1024]{1,0:T(8,128)(2,1)S(1)}, bf16[64,1024]{1,0:T(8,128)(2,1)S(1)}, u32[]{:S(2)}, u32[]{:S(2)}) %collective-permute-start.3) | collective-permute-done | bytes 131104 | tf_op jit(solution)/shard_map/ppermute | solution.py:17
  148.0 8.7 %psum.74 = f32[64]{0:T(128)S(1)} all-reduce(f32[64]{0:T(128)S(1)} %fusion.213), channel_id=1, replica_groups=mesh['section'=4,'dp'=16,'tensor'=4] {'tensor'}, use_global_device_ids=true, to_apply=%region_21.22 | all-reduce | flops 64 | bytes 512 | tf_op jit(solution)/shard_map/psum | solution.py:133
  156.8 8.5 %all_gather.19 = bf16[64,4096]{1,0:T(8,128)(2,1)} all-gather(bf16[64,1024]{1,0:T(8,128)(2,1)S(1)} %fusion.215), channel_id=1, replica_groups=mesh['section'=4,'dp'=16,'tensor'=4] {'tensor'}, dimensions={1}, use_global_device_ids=true | all-gather | bytes 655360 | tf_op jit(solution)/shard_map/all_gather | solution.py:136
  167.5 1.6 select_dynamic-update-slice_fusion.6
  169.1 14.6 %collective-permute-done.4 = bf16[64,1024]{1,0:T(8,128)(2,1)S(1)} collective-permute-done((bf16[64,1024]{1,0:T(8,128)(2,1)S(1)}, bf16[64,1024]{1,0:T(8,128)(2,1)S(1)}, u32[]{:S(2)}, u32[]{:S(2)}) %collective-permute-start.4) | collective-permute-done | bytes 131104 | tf_op jit(solution)/shard_map/ppermute | solution.py:17
  183.8 1.8 collective-permute-start.5
  185.7 3.4 collective-permute-done.5
  192.8 45.6 %reduce-scatter.8.cloned.1.call-done = bf16[64,1024]{1,0:T(8,128)(2,1)} async-done(((bf16[64,4096]{1,0:T(8,128)(2,1)}), bf16[64,1024]{1,0:T(8,128)(2,1)}) %reduce-scatter.8.cloned.1.call-update) | async-done | bytes 131088 | tf_op jit(solution)/shard_map/reduce_scatter | solution.py:198
  239.5 8.4 %psum.75 = f32[64]{0:T(128)S(1)} all-reduce(f32[64]{0:T(128)S(1)} %get-tuple-element.584), channel_id=1, replica_groups=mesh['section'=4,'dp'=16,'tensor'=4] {'tensor'}, use_global_device_ids=true, to_apply=%region_31.32 | all-reduce | flops 64 | bytes 512 | tf_op jit(solution)/shard_map/psum | solution.py:203
  250.0 3.0 collective-permute-start.6
  253.0 2.5 collective-permute-done.6
  256.5 45.2 %reduce-scatter.10.cloned.1.call-done = bf16[64,1024]{1,0:T(8,128)(2,1)} async-done(((bf16[64,4096]{1,0:T(8,128)(2,1)}), bf16[64,1024]{1,0:T(8,128)(2,1)}) %reduce-scatter.10.cloned.1.call-update) | async-done | bytes 131088 | tf_op jit(solution)/shard_map/reduce_scatter | solution.py:198
  302.8 8.4 %psum.76 = f32[64]{0:T(128)S(1)} all-reduce(f32[64]{0:T(128)S(1)} %get-tuple-element.586), channel_id=1, replica_groups=mesh['section'=4,'dp'=16,'tensor'=4] {'tensor'}, use_global_device_ids=true, to_apply=%region_38.39 | all-reduce | flops 64 | bytes 512 | tf_op jit(solution)/shard_map/psum | solution.py:203
  312.2 2.8 collective-permute-start.7
  315.0 2.5 collective-permute-done.7
  322.2 44.1 %reduce-scatter.12.cloned.1.call-done = bf16[64,1024]{1,0:T(8,128)(2,1)} async-done(((bf16[64,4096]{1,0:T(8,128)(2,1)}), bf16[64,1024]{1,0:T(8,128)(2,1)}) %reduce-scatter.12.cloned.1.call-update) | async-done | bytes 131088 | tf_op jit(solution)/shard_map/reduce_scatter | solution.py:198
  367.4 8.3 %psum.77 = f32[64]{0:T(128)S(1)} all-reduce(f32[64]{0:T(128)S(1)} %get-tuple-element.588), channel_id=1, replica_groups=mesh['section'=4,'dp'=16,'tensor'=4] {'tensor'}, use_global_device_ids=true, to_apply=%region_45.46 | all-reduce | flops 64 | bytes 512 | tf_op jit(solution)/shard_map/psum | solution.py:203
  377.6 2.8 collective-permute-start.8
  382.9 18.9 %conditional.18 = (bf16[64,4096]{1,0:T(8,128)(2,1)}, bf16[1,64,1024]{2,1,0:T(8,128)(2,1)}, bf16[1,64,256]{2,1,0:T(8,128)(2,1)S(1)}) conditional(s32[]{:T(128)} %convert_element_type.644, () %tuple.188, (bf16[2,64,256]{2,1,0:T(8,128)(2,1)S(1)}, s32[]{:T(128)}, s32[1,2,64]{2,1,0:T(2,128)}, bf16[2,64,1024]{2,1,0:T(8,128)(2,1)}, ...), branch_computations={%region_46.47_spmd, %region_47.50_spmd} | conditional | flops 714132480 | bytes 25760632 | solution.py:197
  389.6 1.7 copy.189
  392.5 1.6 broadcast_in_dim.371
  394.1 6.1 fusion.136
  404.3 30.0 %reduce-scatter.14.cloned.1.call-done = bf16[64,1024]{1,0:T(8,128)(2,1)} async-done(((bf16[64,4096]{1,0:T(8,128)(2,1)}), bf16[64,1024]{1,0:T(8,128)(2,1)}) %reduce-scatter.14.cloned.1.call-update) | async-done | bytes 131088 | tf_op jit(solution)/shard_map/reduce_scatter | solution.py:198
  434.3 1.6 fusion.232
  436.0 8.3 %psum.78 = f32[64]{0:T(128)S(1)} all-reduce(f32[64]{0:T(128)S(1)} %get-tuple-element.590), channel_id=1, replica_groups=mesh['section'=4,'dp'=16,'tensor'=4] {'tensor'}, use_global_device_ids=true, to_apply=%region_52.53 | all-reduce | flops 64 | bytes 512 | tf_op jit(solution)/shard_map/psum | solution.py:203
  445.0 1.8 fusion.242
  446.8 2.7 collective-permute-start.9
  449.6 2.5 collective-permute-done.9
  452.1 21.4 %conditional.19 = (bf16[64,4096]{1,0:T(8,128)(2,1)}, bf16[1,64,1024]{2,1,0:T(8,128)(2,1)}, bf16[1,64,256]{2,1,0:T(8,128)(2,1)}) conditional(s32[]{:T(128)} %convert_element_type.651, () %tuple.190, (bf16[2,64,256]{2,1,0:T(8,128)(2,1)S(1)}, s32[]{:T(128)}, s32[1,2,64]{2,1,0:T(2,128)}, bf16[2,64,1024]{2,1,0:T(8,128)(2,1)}, ...), branch_computations={%region_53.54_spmd, %region_54.57_spmd} | conditional | flops 714132480 | bytes 25891732 | solution.py:197
  455.5 1.7 fusion.158
  459.5 1.7 copy.200
  465.8 6.0 fusion.161
  479.0 3.0 fusion.175
  484.4 5.6 bitcast_convert_fusion
  491.3 13.9 %reduce-scatter.20.cloned.1.call-done = bf16[64,1024]{1,0:T(8,128)(2,1)} async-done(((bf16[64,4096]{1,0:T(8,128)(2,1)}), bf16[64,1024]{1,0:T(8,128)(2,1)}) %reduce-scatter.20.cloned.1.call-update) | async-done | bytes 131088 | tf_op jit(solution)/shard_map/reduce_scatter | solution.py:198
  506.4 8.3 %psum.79 = f32[64]{0:T(128)S(1)} all-reduce(f32[64]{0:T(128)S(1)} %get-tuple-element.581), channel_id=1, replica_groups=mesh['section'=4,'dp'=16,'tensor'=4] {'tensor'}, use_global_device_ids=true, to_apply=%region_67.68 | all-reduce | flops 64 | bytes 512 | tf_op jit(solution)/shard_map/psum | solution.py:203
  514.7 32.7 %all-reduce = bf16[1024]{0:T(1024)(128)(2,1)S(1)} all-reduce(bf16[1024]{0:T(1024)(128)(2,1)S(1)} %add_convert_fusion), channel_id=9, replica_groups=mesh['section'=4,'dp'=16,'tensor'=4] {'dp'}, use_global_device_ids=true, to_apply=%region_65.66.clone | all-reduce | flops 1024 | bytes 4096
  549.2 32.1 %reduce-scatter.18.cloned.1.call-done = bf16[256,256]{1,0:T(8,128)(2,1)} async-done(((bf16[4096,256]{1,0:T(8,128)(2,1)}), bf16[256,256]{1,0:T(8,128)(2,1)}) %reduce-scatter.18.cloned.1.call-update) | async-done | bytes 131088 | tf_op jit(solution)/shard_map/reduce_scatter | solution.py:227
  581.3 1.6 bitcast_convert_fusion.2
  582.9 183.6 %reduce-scatter.16.cloned.1.call-done = bf16[256,1024]{1,0:T(8,128)(2,1)} async-done(((bf16[4096,1024]{1,0:T(8,128)(2,1)}), bf16[256,1024]{1,0:T(8,128)(2,1)}) %reduce-scatter.16.cloned.1.call-update) | async-done | bytes 524304 | tf_op jit(solution)/shard_map/reduce_scatter | solution.py:224
  766.5 2.1 bitcast_convert_fusion.1
  (234 shorter events, 78.8 us)
Async XLA Ops:
  7.2 231.2 %reduce-scatter.8.cloned.1.call-start = ((), (), s32[]{:S(2)}) async-start(), calls=%async_computation.7 | async-start | bytes 655360 | tf_op jit(solution)/shard_map/reduce_scatter | solution.py:198
  27.5 11.9 %copy-start.10 = (bf16[1,2,64,1024]{3,2,1,0:T(8,128)(2,1)S(1)}, bf16[1,2,64,1024]{3,2,1,0:T(8,128)(2,1)}, u32[]{:S(2)}) copy-start(bf16[1,2,64,1024]{3,2,1,0:T(8,128)(2,1)} %param.30) | copy-start | bytes 786436
  39.5 7.0 collective-permute-start
  75.0 7.0 collective-permute-start.1
  100.5 13.2 %collective-permute-start.2 = (bf16[64,1024]{1,0:T(8,128)(2,1)S(1)}, bf16[64,1024]{1,0:T(8,128)(2,1)S(1)}, u32[]{:S(2)}, u32[]{:S(2)}) collective-permute-start(bf16[64,1024]{1,0:T(8,128)(2,1)S(1)} %fusion.208), channel_id=1, source_target_pairs={{0,64},{64,128},{128,192},{192,0},{1,65},{65,129},{129,193},{193,1... | collective-permute-start | bytes 393224 | tf_op jit(solution)/shard_map/ppermute | solution.py:17
  132.0 15.9 %collective-permute-start.3 = (bf16[64,1024]{1,0:T(8,128)(2,1)S(1)}, bf16[64,1024]{1,0:T(8,128)(2,1)S(1)}, u32[]{:S(2)}, u32[]{:S(2)}) collective-permute-start(bf16[64,1024]{1,0:T(8,128)(2,1)S(1)} %fusion.212), channel_id=1, source_target_pairs={{0,64},{64,128},{128,192},{192,0},{1,65},{65,129},{129,193},{193,1... | collective-permute-start | bytes 393224 | tf_op jit(solution)/shard_map/ppermute | solution.py:17
  156.7 8.6 %copy-start.31 = (f32[64]{0:T(128)}, f32[64]{0:T(128)S(1)}, u32[]{:S(2)}) copy-start(f32[64]{0:T(128)S(1)} %psum.74) | copy-start | bytes 772
  165.3 18.4 %copy-start.20 = (bf16[1,2,64,1024]{3,2,1,0:T(8,128)(2,1)S(1)}, bf16[1,2,64,1024]{3,2,1,0:T(8,128)(2,1)}, u32[]{:S(2)}) copy-start(bf16[1,2,64,1024]{3,2,1,0:T(8,128)(2,1)} %param.31) | copy-start | bytes 786436
  166.7 17.1 %collective-permute-start.4 = (bf16[64,1024]{1,0:T(8,128)(2,1)S(1)}, bf16[64,1024]{1,0:T(8,128)(2,1)S(1)}, u32[]{:S(2)}, u32[]{:S(2)}) collective-permute-start(bf16[64,1024]{1,0:T(8,128)(2,1)S(1)} %fusion.216), channel_id=1, source_target_pairs={{0,64},{64,128},{128,192},{192,0},{1,65},{65,129},{129,193},{193,1... | collective-permute-start | bytes 393224 | tf_op jit(solution)/shard_map/ppermute | solution.py:17
  183.8 5.9 copy-start.14
  183.8 5.3 collective-permute-start.5
  189.1 0.6 copy-start.22
  190.4 0.8 copy-start.7
  190.4 65.1 %copy-start.26 = (bf16[1,64,256]{2,1,0:T(8,128)(2,1)}, bf16[1,64,256]{2,1,0:T(8,128)(2,1)S(1)}, u32[]{:S(2)}) copy-start(bf16[1,64,256]{2,1,0:T(8,128)(2,1)S(1)} %get-tuple-element.575) | copy-start | bytes 98308
  191.3 110.4 %reduce-scatter.10.cloned.1.call-start = ((), (), s32[]{:S(2)}) async-start(), calls=%async_computation.8 | async-start | bytes 655360 | tf_op jit(solution)/shard_map/reduce_scatter | solution.py:198
  250.0 5.5 collective-permute-start.6
  255.6 0.8 copy-start.8
  255.6 62.6 %copy-start.15 = (bf16[1,64,1024]{2,1,0:T(8,128)(2,1)}, bf16[1,64,1024]{2,1,0:T(8,128)(2,1)S(1)}, u32[]{:S(2)}) copy-start(bf16[1,64,1024]{2,1,0:T(8,128)(2,1)S(1)} %get-tuple-element.568) | copy-start | bytes 393220
  255.6 62.6 %copy-start.24 = (bf16[1,64,256]{2,1,0:T(8,128)(2,1)}, bf16[1,64,256]{2,1,0:T(8,128)(2,1)S(1)}, u32[]{:S(2)}) copy-start(bf16[1,64,256]{2,1,0:T(8,128)(2,1)S(1)} %get-tuple-element.576) | copy-start | bytes 98308
  256.4 109.9 %reduce-scatter.12.cloned.1.call-start = ((), (), s32[]{:S(2)}) async-start(), calls=%async_computation.9 | async-start | bytes 655360 | tf_op jit(solution)/shard_map/reduce_scatter | solution.py:198
  312.2 5.3 collective-permute-start.7
  317.5 0.7 copy-start.27
  318.8 0.8 copy-start.9
  318.9 64.1 %copy-start.16 = (bf16[1,64,1024]{2,1,0:T(8,128)(2,1)}, bf16[1,64,1024]{2,1,0:T(8,128)(2,1)S(1)}, u32[]{:S(2)}) copy-start(bf16[1,64,1024]{2,1,0:T(8,128)(2,1)S(1)} %get-tuple-element.570) | copy-start | bytes 393220
  319.7 114.7 %reduce-scatter.14.cloned.1.call-start = ((), (), s32[]{:S(2)}) async-start(), calls=%async_computation.10 | async-start | bytes 655360 | tf_op jit(solution)/shard_map/reduce_scatter | solution.py:198
  377.6 5.4 copy-start.5
  377.6 5.3 collective-permute-start.8
  383.3 16.9 %copy-start.3 = (bf16[4096,256]{1,0:T(8,128)(2,1)S(1)}, bf16[4096,256]{1,0:T(8,128)(2,1)}, u32[]{:S(2)}) copy-start(bf16[4096,256]{1,0:T(8,128)(2,1)} %get-tuple-element.509) | copy-start | bytes 6291460 | tf_op jit(solution)/shard_map/cond
  385.2 2.7 copy-start.17
  387.9 0.7 copy-start.11
  401.8 47.7 %copy-start.25 = (bf16[1,64,256]{2,1,0:T(8,128)(2,1)}, bf16[1,64,256]{2,1,0:T(8,128)(2,1)S(1)}, u32[]{:S(2)}) copy-start(bf16[1,64,256]{2,1,0:T(8,128)(2,1)S(1)} %get-tuple-element.578) | copy-start | bytes 98308
  401.8 103.4 %reduce-scatter.20.cloned.1.call-start = ((), (), s32[]{:S(2)}) async-start(), calls=%async_computation.13 | async-start | bytes 655360 | tf_op jit(solution)/shard_map/reduce_scatter | solution.py:198
  446.8 5.2 collective-permute-start.9
  449.6 2.5 copy-start.13
  452.1 19.8 %copy-start.4 = (bf16[4096,256]{1,0:T(8,128)(2,1)S(1)}, bf16[4096,256]{1,0:T(8,128)(2,1)}, u32[]{:S(2)}) copy-start(bf16[4096,256]{1,0:T(8,128)(2,1)} %get-tuple-element.516) | copy-start | bytes 6291460 | tf_op jit(solution)/shard_map/cond
  455.1 3.3 copy-start.18
  458.5 0.6 copy-start.12
  465.8 6.1 copy-start.19
  473.5 107.9 %reduce-scatter.18.cloned.1.call-start = ((), (), s32[]{:S(2)}) async-start(), calls=%async_computation.12 | async-start | bytes 2228224 | tf_op jit(solution)/shard_map/reduce_scatter | solution.py:227
  482.0 284.5 %reduce-scatter.16.cloned.1.call-start = ((), (), s32[]{:S(2)}) async-start(), calls=%async_computation.11 | async-start | bytes 8912896 | tf_op jit(solution)/shard_map/reduce_scatter | solution.py:224
  484.4 5.7 copy-start.32
  484.4 6.9 copy-start.6
  484.4 20.9 %copy-start.30 = (f32[64]{0:T(128)S(1)}, f32[64]{0:T(128)}, u32[]{:S(2)}) copy-start(f32[64]{0:T(128)} %get-tuple-element.651) | copy-start | bytes 772
  484.4 30.3 %copy-start.29 = (f32[1024]{0:T(1024)S(1)}, f32[1024]{0:T(1024)}, u32[]{:S(2)}) copy-start(f32[1024]{0:T(1024)} %get-tuple-element.589) | copy-start | bytes 12292
  549.2 219.5 %copy-start.21 = (bf16[1,1,2,64,1024]{4,3,2,1,0:T(8,128)(2,1)}, bf16[1,1,2,64,1024]{4,3,2,1,0:T(8,128)(2,1)S(1)}, u32[]{:S(2)}) copy-start(bf16[1,1,2,64,1024]{4,3,2,1,0:T(8,128)(2,1)S(1)} %fusion.239) | copy-start | bytes 786436
Sparse Core Ops, SparseCore 0:
  191.4 46.9 reduce-scatter.7
  256.5 45.0 reduce-scatter.9
  319.8 46.4 reduce-scatter.11
  402.0 32.3 reduce-scatter.13
  473.6 31.6 reduce-scatter.19
  507.8 73.4 reduce-scatter.17
  584.0 182.4 reduce-scatter.15
where the time goes:
time: 788 us; the launch traced here: 776 us
  waiting for transfers between devices  443 us (56%)
  blocking collectives  159 us (20%)
  matrix products  52.5 us (7%)
  other arithmetic  48.2 us (6%)
  local copies, waits for them, and re-layouts  29.6 us (4%)
  starting transfers between devices  27.2 us (3%)
  between operations  15.6 us (2%)
    reduce_scatter x1, waiting for transfers between devices, body(): lax.psum_scatter(term_query.astype(jnp.bfloat16), 'dp', scatter_dimension...  184 us
    reduce_scatter x5, waiting for transfers between devices, body(): lax.psum_scatter(results[2].astype(jnp.bfloat16), 'tensor', scatter_dimen...  179 us
    ppermute x10, waiting for transfers between devices, passed_along(): lax.ppermute(array, axis, [(i, (i + by) % length) for i in range(length)])  48.3 us
    all_gather x5, blocking collectives, body(): normalize_gathered = lax.all_gather(normed, 'tensor', axis=1, tiled=True)  42.4 us
    psum x5, blocking collectives, body(): lax.psum(jnp.sum(normalize_widened * normalize_widened, axis=1), 'tensor')  41.9 us
    psum x5, blocking collectives, body(): row_dots = lax.psum(jnp.sum(scaled * widened, axis=1), 'tensor')  41.8 us
    unnamed x1, blocking collectives  32.7 us
    reduce_scatter x1, waiting for transfers between devices, body(): lax.psum_scatter(term_keyval.astype(jnp.bfloat16), 'dp', scatter_dimensio...  32.1 us
  transfers between devices with their start and end apart: 17, of which 17 were waited for; matrix products, arithmetic and copies ran while one was open for 5% of the time, Pallas kernels for 0%

commit v1 on v0

v1 whole, which is shorter than its diff:
```python
import math

import jax
import jax.numpy as jnp
from jax import lax
from jax.experimental import pallas as pl
from jax.experimental.pallas import tpu as pltpu
from jax.sharding import PartitionSpec as P

EPSILON = 1e-05
D = 4096
HD = 128
L = 64
MB = 2
DP = 16
SECTIONS = 4
TENSOR = 4
ROWS = D // DP
QC = 1024
KC = 256
C = QC + KC
BLK = 1024
HB = BLK // 2
BF = jnp.bfloat16
F32 = jnp.float32
MESH = pl.DeviceIdType.MESH
SCALE = 1.0 / math.sqrt(HD)
NT = (((1,), (1,)), ((), ()))
TN = (((0,), (0,)), ((), ()))
NN = (((1,), (0,)), ((), ()))


def dot(a, b, dims=NN):
    return lax.dot_general(a, b, dims, preferred_element_type=F32)


def stack_heads(x):
    return jnp.concatenate([x[:, i * HD : (i + 1) * HD] for i in range(x.shape[1] // HD)], axis=0)


def unstack_heads(x):
    return jnp.concatenate([x[i * L : (i + 1) * L] for i in range(x.shape[0] // L)], axis=1)


def kernel(
    hid, tea, seg, wq, wkv, gain,
    o_gq, o_gkv, o_gg, o_lig,
    w, hbuf, g16, acc, qkv, probs, mask, invb, outb, dyb,
    usend, uall, dqall, msend, mrecv, bsend, asend, abuf, bbuf, bfin, lig, gtot, ggsend, ggrecv,
    w_sem, g_ssem, g_rsem, h_ssem, h_rsem, u_ssem, u_rsem, q_ssem, q_rsem,
    m_ssem, m_rsem, ab_ssem, a_rsem, b_rsem, f_rsem, l_ssem, l_rsem, gg_ssem, gg_rsem,
):
    s = lax.axis_index("section")
    d = lax.axis_index("dp")
    t = lax.axis_index("tensor")
    t1 = t + 1 - 2 * lax.rem(t, 2)
    t2 = lax.rem(t + 2, 4)
    t3 = 3 - t
    z = d // 2
    xl = lax.rem(d, 2)
    sn = lax.rem(s + 1, SECTIONS)
    sp = lax.rem(s + SECTIONS - 1, SECTIONS)

    def rcopy(src, dst, ssem, rsem, dev):
        return pltpu.make_async_remote_copy(
            src_ref=src, dst_ref=dst, send_sem=ssem, recv_sem=rsem, device_id=dev, device_id_type=MESH
        )

    bar = pltpu.get_barrier_semaphore()
    for dev in ((s, d, t1), (s, d, t2), (s, d, t3), (sn, d, t), (sn, d, t2), (sp, d, t), (sp, d, t2)):
        pl.semaphore_signal(bar, inc=1, device_id=dev, device_id_type=MESH)

    def greet(i, _):
        pl.semaphore_signal(bar, inc=1, device_id=(s, lax.rem(d + i, DP), t), device_id_type=MESH)
        return 0

    lax.fori_loop(1, DP, greet, 0)
    gt = d // 4
    src_d = 4 * t + d // 4
    quarter = lax.rem(d, 4)
    loop = (gt == t) & (quarter == gt)
    for tt in range(TENSOR):
        @pl.when(jnp.logical_not(loop & (tt == t)))
        def _():
            pl.semaphore_signal(bar, inc=1, device_id=(s, src_d, tt), device_id_type=MESH)

    def w_copies(j):
        rows = pl.ds(pl.multiple_of(j * BLK, BLK), BLK)
        return (
            pltpu.make_async_copy(wq.at[0, rows, :], w.at[rows, pl.ds(0, QC)], w_sem.at[0, j]),
            pltpu.make_async_copy(wkv.at[0, rows, :], w.at[rows, pl.ds(QC, KC)], w_sem.at[1, j]),
        )

    for j in (t, t1, t2, t3):
        for c in w_copies(j):
            c.start()

    ri = lax.broadcasted_iota(jnp.int32, (L, L), 0)
    ci = lax.broadcasted_iota(jnp.int32, (L, L), 1)
    for m in range(MB):
        srow = jnp.broadcast_to(seg[0, m : m + 1, :], (L, L))
        scol = jnp.sum(jnp.where(ri == ci, srow, 0), axis=1, keepdims=True)
        mask[m] = jnp.where((srow == scol) & (ri >= ci), 1.0, 0.0)
    for i in range(4):
        g16[4 * t + i] = jnp.broadcast_to(gain[:, i * ROWS : (i + 1) * ROWS].astype(F32), (8, ROWS))

    pl.semaphore_wait(bar, 26 - jnp.where(loop, 1, 0))

    def g_copy(i, dev_t):
        sl = g16.at[pl.ds(4 * t, 4)]
        return rcopy(sl, sl, g_ssem.at[i], g_rsem.at[t], (s, d, dev_t))

    def h_copy(m, k, kind, slot, src, dev):
        return rcopy(src, hbuf.at[m, slot, k], h_ssem.at[m, kind, k], h_rsem.at[m, slot, k], dev)

    for i, tt in enumerate((t1, t2, t3)):
        g_copy(i, tt).start()

    @pl.when(s == 0)
    def _():
        for m in range(MB):
            for k in range(2):
                hbuf[m, t, k] = hid[0, m, :, k * HB : (k + 1) * HB]
                h_copy(m, k, 4, t, hbuf.at[m, t, k], (s, d, t2)).start()

    for tt in (t1, t2, t3):
        sl = g16.at[pl.ds(4 * tt, 4)]
        rcopy(sl, sl, g_ssem.at[0], g_rsem.at[tt], (s, d, tt)).wait_recv()

    def gains(j, k):
        p = 4 * j + 2 * k
        return jnp.concatenate([g16[p, 0:1, :], g16[p + 1, 0:1, :]], axis=1)

    def h_wait(m, slot, k):
        h_copy(m, k, 0, slot, hbuf.at[m, slot, k], (s, d, t1)).wait_recv()

    def forward(m):
        ss = jnp.zeros((L, 1), F32)

        def kstep(j, k, first):
            x = hbuf[m, j, k].astype(F32)
            part_ss = jnp.sum(x * x, axis=1, keepdims=True)
            xg = (x * gains(j, k)).astype(BF)
            part = dot(xg, w[pl.ds(pl.multiple_of(j * BLK + k * HB, HB), HB), :])
            if first:
                acc[...] = part
            else:
                acc[...] += part
            return part_ss

        def need_w(j):
            if m == 0:
                for c in w_copies(j):
                    c.wait()

        for k in range(2):
            @pl.when(s > 0)
            def _():
                h_wait(m, t, k)
            h_copy(m, k, 2, t, hbuf.at[m, t, k], (s, d, t1)).start()
        need_w(t)
        for k in range(2):
            ss += kstep(t, k, k == 0)
        for k in range(2):
            h_wait(m, t2, k)
            h_copy(m, k, 3, t2, hbuf.at[m, t2, k], (s, d, t1)).start()
        need_w(t1)
        for k in range(2):
            h_wait(m, t1, k)
            ss += kstep(t1, k, False)
        need_w(t2)
        for k in range(2):
            ss += kstep(t2, k, False)
        need_w(t3)
        for k in range(2):
            h_wait(m, t3, k)
            ss += kstep(t3, k, False)
        inv = lax.rsqrt(ss / D + EPSILON)
        invb[m] = jnp.broadcast_to(inv, (L, 128))
        qkv[m] = (acc[...] * inv).astype(BF)
        key = qkv[m, :, QC : QC + HD]
        val = qkv[m, :, QC + HD :]
        allowed = jnp.concatenate([mask[m]] * 4, axis=0) > 0.0
        for k in range(2):
            q = stack_heads(qkv[m, :, k * HB : (k + 1) * HB])
            sc = dot(q, key, NT) * SCALE
            e = jnp.exp(jnp.where(allowed, sc, -1e30))
            pr = e / jnp.sum(e, axis=1, keepdims=True)
            probs[m, k] = pr
            o = dot(pr.astype(BF), val).astype(BF)
            hn = (hbuf[m, t, k].astype(F32) + unstack_heads(o).astype(F32)).astype(BF)
            outb[m, k] = hn

            @pl.when(s < SECTIONS - 1)
            def _():
                h_copy(m, k, 0, t, outb.at[m, k], (sn, d, t)).start()
                h_copy(m, k, 1, t, outb.at[m, k], (sn, d, t2)).start()

            @pl.when(s == SECTIONS - 1)
            def _():
                dyb[m, k] = (
                    hn.astype(F32) - tea[0, m, :, k * HB : (k + 1) * HB].astype(F32)
                ).astype(BF)

    def u_copy(m, i):
        p = lax.rem(d + i, DP)
        return rcopy(usend.at[m, p], uall.at[m, d], u_ssem.at[m, i], u_rsem.at[m, d], (s, p, t))

    def send_rows(m):
        inv = invb[m, :, 0:1]
        for j in range(TENSOR):
            for k in range(2):
                u = (hbuf[m, j, k].astype(F32) * inv).astype(BF)
                usend[m, 4 * j + 2 * k] = u[:, :ROWS]
                usend[m, 4 * j + 2 * k + 1] = u[:, ROWS:]
        uall[m, d] = usend[m, d]

        def one(i, _):
            u_copy(m, i).start()
            return 0

        lax.fori_loop(1, DP, one, 0)

    def q_copy(m, src_d, sem, dev_d):
        blk = dqall.at[m, src_d]
        return rcopy(blk, blk, q_ssem.at[m, sem], q_rsem.at[m, src_d], (s, dev_d, t))

    dx = d + 1 - 2 * xl
    zr = lax.rem(z + 1, 8)
    zl = lax.rem(z + 7, 8)

    def q_start(m):
        q_copy(m, d, 0, dx).start()
        q_copy(m, d, 1, 2 * zr + xl).start()
        q_copy(m, d, 2, 2 * zl + xl).start()

    def q_wait(m, src_d):
        q_copy(m, src_d, 0, dx).wait_recv()

    def q_hop(m, r, col):
        cx = xl if col == 0 else 1 - xl
        right = 2 * lax.rem(z + 8 - r, 8) + cx
        left = 2 * lax.rem(z + r, 8) + cx
        sem = 1 + 4 * r + 2 * col
        if r > 0 or col == 1:
            q_wait(m, right)
            if r > 0:
                q_wait(m, left)
            if r < 3 or col == 0:
                q_copy(m, right, sem, 2 * zr + xl).start()
            if r < 3 or col == 1:
                q_copy(m, left, sem + 1, 2 * zl + xl).start()

    def q_finish(m):
        for col in range(2):
            q_wait(m, 2 * lax.rem(z + 4, 8) + (xl if col == 0 else 1 - xl))

    def q_drain(m):
        q_copy(m, d, 0, dx).wait_send()
        for r in range(4):
            for col in range(2):
                if r < 3 or col == 0:
                    q_copy(m, d, 1 + 4 * r + 2 * col, dx).wait_send()
                if r < 3 or col == 1:
                    q_copy(m, d, 2 + 4 * r + 2 * col, dx).wait_send()

    def m_copy(m, i, k):
        return rcopy(msend.at[m, i, k], mrecv.at[m, i, k], m_ssem.at[m, i, k], m_rsem.at[m, i, k], (s, d, t1))

    def a_copy(m, k):
        return rcopy(asend.at[m, k], abuf.at[m, k], ab_ssem.at[0, m, k], a_rsem.at[m, k], (sp, d, t))

    def b_copy(m, k):
        return rcopy(bsend.at[m, k], bbuf.at[m, k], ab_ssem.at[1, m, k], b_rsem.at[m, k], (sp, d, t2))

    def f_copy(m, k):
        return rcopy(bsend.at[m, k], bfin.at[m, k], ab_ssem.at[1, m, k], f_rsem.at[m, k], (s, d, t2))

    def l_copy(m, k):
        return rcopy(dyb.at[m, k], lig.at[m, k], l_ssem.at[m, k], l_rsem.at[m, k], (sn, d, t))

    def backward(m):
        key = qkv[m, :, QC : QC + HD]
        val = qkv[m, :, QC + HD :]
        inv = invb[m, :, 0:1]
        dk = jnp.zeros((L, HD), F32)
        dv = jnp.zeros((L, HD), F32)
        rd = jnp.zeros((L, 1), F32)
        for k in range(2):
            @pl.when(s < SECTIONS - 1)
            def _():
                a_copy(m, k).wait_recv()
                b_copy(m, k).wait_recv()
                dyb[m, k] = (abuf[m, k].astype(F32) + bbuf[m, k].astype(F32)).astype(BF)
                l_copy(m, k).start()

            do = stack_heads(dyb[m, k])
            q = stack_heads(qkv[m, :, k * HB : (k + 1) * HB])
            pr = probs[m, k]
            dp = dot(do, val, NT)
            ds = (pr * (dp - jnp.sum(dp * pr, axis=1, keepdims=True))).astype(BF)
            dq = (dot(ds, key) * SCALE).astype(BF)
            dqall[m, d, :, k * HB : (k + 1) * HB] = unstack_heads(dq)
            dk += dot(ds, q, TN)
            dv += dot(pr.astype(BF), do, TN)
            qd = jnp.sum(q.astype(F32) * dq.astype(F32), axis=1, keepdims=True)
            for i in range(4):
                rd += qd[i * L : (i + 1) * L]
        dkb = (dk * SCALE).astype(BF)
        dvb = dv.astype(BF)
        dqall[m, d, :, QC : QC + HD] = dkb
        dqall[m, d, :, QC + HD :] = dvb
        rd += jnp.sum(
            key.astype(F32) * dkb.astype(F32) + val.astype(F32) * dvb.astype(F32), axis=1, keepdims=True
        )
        q_start(m)
        coef = inv * inv * rd / D
        grads = dqall[m, d]

        def term(j, k):
            part = dot(grads, w[pl.ds(pl.multiple_of(j * BLK + k * HB, HB), HB), :], NT)
            return inv * gains(j, k) * part - hbuf[m, j, k].astype(F32) * coef

        for i, j in enumerate((t3, t1)):
            for k in range(2):
                msend[m, i, k] = term(j, k).astype(BF)
                m_copy(m, i, k).start()
        for k in range(2):
            own = term(t2, k)
            m_copy(m, 0, k).wait_recv()
            bsend[m, k] = (own + mrecv[m, 0, k].astype(F32)).astype(BF)

            @pl.when(s > 0)
            def _():
                b_copy(m, k).start()

            @pl.when(s == 0)
            def _():
                f_copy(m, k).start()

        for k in range(2):
            own = term(t, k) + dyb[m, k].astype(F32)
            m_copy(m, 1, k).wait_recv()
            asend[m, k] = (own + mrecv[m, 1, k].astype(F32)).astype(BF)

            @pl.when(s > 0)
            def _():
                a_copy(m, k).start()

    for m in range(MB):
        forward(m)
    for m in range(MB):
        send_rows(m)
    for m in range(MB):
        backward(m)

    for r in range(4):
        for m in range(MB):
            for col in range(2):
                q_hop(m, r, col)

    @pl.when(s == 0)
    def _():
        for m in range(MB):
            for k in range(2):
                f_copy(m, k).wait_recv()
                lig[m, k] = (asend[m, k].astype(F32) + bfin[m, k].astype(F32)).astype(BF)

    @pl.when(s > 0)
    def _():
        for m in range(MB):
            for k in range(2):
                l_copy(m, k).wait_recv()

    for m in range(MB):
        for k in range(2):
            o_lig[0, 0, m, :, k * HB : (k + 1) * HB] = lig[m, k]

    for m in range(MB):
        def u_wait(i, _):
            p = lax.rem(d + i, DP)
            rcopy(usend.at[m, p], uall.at[m, p], u_ssem.at[m, i], u_rsem.at[m, p], (s, p, t)).wait_recv()
            return 0

        lax.fori_loop(1, DP, u_wait, 0)
        q_finish(m)
        u = uall[m].reshape(DP * L, ROWS)
        g = dqall[m].reshape(DP * L, C)
        if m == 0:
            gtot[...] = dot(u, g, TN)
        else:
            gtot[...] += dot(u, g, TN)

    eye = lax.broadcasted_iota(jnp.int32, (ROWS, ROWS), 0) == lax.broadcasted_iota(jnp.int32, (ROWS, ROWS), 1)
    total = gtot[...]
    rows = pl.ds(pl.multiple_of(d * ROWS, ROWS), ROWS)
    col = jnp.sum(total * w[rows, :].astype(F32), axis=1, keepdims=True)
    row = jnp.sum(jnp.where(eye, jnp.broadcast_to(col, (ROWS, ROWS)), 0.0), axis=0, keepdims=True)
    ggsend[...] = jnp.broadcast_to(row, (8, ROWS))

    def gg_copy(j):
        return rcopy(ggsend, ggrecv.at[t], gg_ssem.at[j], gg_rsem.at[t], (s, 4 * quarter + j, gt))

    for j in range(4):
        mine = loop & (quarter == j)

        @pl.when(jnp.logical_not(mine))
        def _():
            gg_copy(j).start()

        @pl.when(mine)
        def _():
            ggrecv[t] = ggsend[...]

    gcol = jnp.sum(
        jnp.where(eye, jnp.broadcast_to(g16[d, 0:1, :], (ROWS, ROWS)), 0.0), axis=1, keepdims=True
    )
    o_gq[0] = total[:, :QC] * gcol
    o_gkv[0] = total[:, QC:] * gcol

    for tt in range(TENSOR):
        @pl.when(jnp.logical_not(loop & (tt == t)))
        def _():
            rcopy(ggsend, ggrecv.at[tt], gg_ssem.at[0], gg_rsem.at[tt], (s, src_d, tt)).wait_recv()
    gsum = ggrecv[0] + ggrecv[1] + ggrecv[2] + ggrecv[3]
    picked = jnp.zeros((1, L), F32)
    for j in range(4):
        picked += jnp.where(quarter == j, 1.0, 0.0) * gsum[0:1, j * L : (j + 1) * L]
    o_gg[...] = picked

    for i, tt in enumerate((t1, t2, t3)):
        g_copy(i, tt).wait_send()
    for m in range(MB):
        for k in range(2):
            h_copy(m, k, 2, t, hbuf.at[m, t, k], (s, d, t1)).wait_send()
            h_copy(m, k, 3, t2, hbuf.at[m, t2, k], (s, d, t1)).wait_send()

            @pl.when(s == 0)
            def _():
                h_copy(m, k, 4, t, hbuf.at[m, t, k], (s, d, t2)).wait_send()

            @pl.when(s < SECTIONS - 1)
            def _():
                h_copy(m, k, 0, t, outb.at[m, k], (sn, d, t)).wait_send()
                h_copy(m, k, 1, t, outb.at[m, k], (sn, d, t2)).wait_send()
                l_copy(m, k).wait_send()

            for i in range(2):
                m_copy(m, i, k).wait_send()
            b_copy(m, k).wait_send()

            @pl.when(s > 0)
            def _():
                a_copy(m, k).wait_send()

        def u_drain(i, _):
            u_copy(m, i).wait_send()
            return 0

        lax.fori_loop(1, DP, u_drain, 0)
        q_drain(m)
    for j in range(4):
        mine = loop & (quarter == j)

        @pl.when(jnp.logical_not(mine))
        def _():
            gg_copy(j).wait_send()


def body(hidden_in, teacher, segment_ids, w_query, w_keyval, norm_gain):
    vmem = pl.BlockSpec(memory_space=pltpu.VMEM)
    hbm = pl.BlockSpec(memory_space=pl.ANY)
    dma = pltpu.SemaphoreType.DMA
    V = pltpu.VMEM
    out = pl.pallas_call(
        kernel,
        out_shape=(
            jax.ShapeDtypeStruct((1, ROWS, QC), F32),
            jax.ShapeDtypeStruct((1, ROWS, KC), F32),
            jax.ShapeDtypeStruct((1, L), F32),
            jax.ShapeDtypeStruct((1, 1, MB, L, BLK), BF),
        ),
        in_specs=[vmem, vmem, vmem, hbm, hbm, vmem],
        out_specs=(vmem, vmem, vmem, vmem),
        scratch_shapes=[
            V((D, C), BF),
            V((MB, TENSOR, 2, L, HB), BF),
            V((DP, 8, ROWS), F32),
            V((L, C), F32),
            V((MB, L, C), BF),
            V((MB, 2, 4 * L, L), F32),
            V((MB, L, L), F32),
            V((MB, L, 128), F32),
            V((MB, 2, L, HB), BF),
            V((MB, 2, L, HB), BF),
            V((MB, DP, L, ROWS), BF),
            V((MB, DP, L, ROWS), BF),
            V((MB, DP, L, C), BF),
            V((MB, 2, 2, L, HB), BF),
            V((MB, 2, 2, L, HB), BF),
            V((MB, 2, L, HB), BF),
            V((MB, 2, L, HB), BF),
            V((MB, 2, L, HB), BF),
            V((MB, 2, L, HB), BF),
            V((MB, 2, L, HB), BF),
            V((MB, 2, L, HB), BF),
            V((ROWS, C), F32),
            V((8, ROWS), F32),
            V((TENSOR, 8, ROWS), F32),
            dma((2, TENSOR)),
            dma((3,)),
            dma((TENSOR,)),
            dma((MB, 5, 2)),
            dma((MB, TENSOR, 2)),
            dma((MB, DP)),
            dma((MB, DP)),
            dma((MB, 17)),
            dma((MB, DP)),
            dma((MB, 2, 2)),
            dma((MB, 2, 2)),
            dma((2, MB, 2)),
            dma((MB, 2)),
            dma((MB, 2)),
            dma((MB, 2)),
            dma((MB, 2)),
            dma((MB, 2)),
            dma((4,)),
            dma((TENSOR,)),
        ],
        compiler_params=pltpu.CompilerParams(
            collective_id=1, has_side_effects=True, vmem_limit_bytes=58 * 1024 * 1024
        ),
        name="train_step",
    )(hidden_in, teacher, segment_ids, w_query, w_keyval, norm_gain)
    return out


def solution(mesh):
    in_specs = (
        P("dp", None, None, "tensor"),
        P("dp", None, None, "tensor"),
        P("dp", None, None),
        P("section", None, "tensor"),
        P("section", None, "tensor"),
        P("section", "tensor"),
    )
    out_specs = (
        P("section", "dp", "tensor"),
        P("section", "dp", "tensor"),
        P("section", ("tensor", "dp")),
        P("section", "dp", None, None, "tensor"),
    )
    return jax.shard_map(body, mesh=mesh, in_specs=in_specs, out_specs=out_specs, check_vma=False)
```

time: 788 us -> 176 us (0.22); the launches traced: 776 us -> 173 us
  waiting for transfers between devices: 443 us -> 0 us
  Pallas kernels: 0 us -> 166 us
  blocking collectives: 159 us -> 0 us
  matrix products: 52.5 us -> 0 us
  other arithmetic: 48.2 us -> 0 us
  starting transfers between devices: 27.2 us -> 0 us
  local copies, waits for them, and re-layouts: 29.6 us -> 6.83 us
  between operations: 15.6 us -> 0.64 us
    reduce_scatter x7 -> x0, waiting for transfers between devices: 394 us -> none  [the longest x1 184 us: body(): lax.psum_scatter(term_query.astype(jnp.bfloat16), 'dp', scatter_dimension...]
    pallas_call x0 -> x1, Pallas kernels: none -> 166 us  [body(): pl.pallas_call(kernel, out_shape=(jax.ShapeDtypeStruct((1, ROWS, QC), F32...]
    psum x10 -> x0, blocking collectives: 83.6 us -> none  [the longest x5 41.9 us: body(): lax.psum(jnp.sum(normalize_widened * normalize_widened, axis=1), 'tensor')]
    dot_general x24 -> x0, matrix products: 52.5 us -> none  [the longest x2 12.2 us: local_backward(): jnp.einsum('lc,dc->ld', grad_query, query_proj, preferred_element_type=jn...]
    ppermute x10 -> x0, waiting for transfers between devices: 48.3 us -> none  [passed_along(): lax.ppermute(array, axis, [(i, (i + by) % length) for i in range(length)])]
    all_gather x5 -> x0, blocking collectives: 42.4 us -> none  [body(): normalize_gathered = lax.all_gather(normed, 'tensor', axis=1, tiled=True)]
    unnamed x1 -> x0, blocking collectives: 32.7 us -> none
    select_n x42 -> x0, other arithmetic: 31.4 us -> none  [the longest x40 30.4 us: keep_slot(): return jnp.where(active, updated, store)]
  transfers between devices with their start and end apart: 17 -> 0, of which waited for: 17 -> 0; matrix products, arithmetic and copies ran while one was open for 5% -> 0% of each run, Pallas kernels for 0% -> 0%
where the time goes in v1:
time: 176 us; the launch traced here: 173 us
  Pallas kernels  166 us (94%)
  local copies, waits for them, and re-layouts  6.83 us (4%)
    pallas_call x1, Pallas kernels, body(): pl.pallas_call(kernel, out_shape=(jax.ShapeDtypeStruct((1, ROWS, QC), F32...  166 us
    unnamed x4, local copies, waits for them, and re-layouts  6.83 us

profile of v1, /device:TPU:2, one launch (start us, length us, event | category | flops | bytes accessed | tf_op | source)
XLA Modules:
  0.0 173.0 jit_solution(9583581596031207673)
XLA Ops:
  0.6 165.6 %train_step.1 = (f32[1,256,1024]{2,1,0:T(8,128)}, f32[1,256,256]{2,1,0:T(8,128)}, f32[1,64]{1,0:T(1,128)}, bf16[1,1,2,64,1024]{4,3,2,1,0:T(8,128)(2,1)}) custom-call(bf16[1,2,64,1024]{3,2,1,0:T(8,128)(2,1)} %hid.1, bf16[1,2,64,1024]{3,2,1,0:T(8,128)(2,1)} %tea.1, s32[1,2,64]{2,1,0:T(2,128)} %seg.1, bf16[1,4096,1024]{2,1,0:T(8,128)(2,1)} %wq.1, ...), custom_call_target="tpu_custom_call" | custom-call | tf_op jit(solution)/shard_map/train_step/pallas_call | solution.py:475
  166.2 2.3 %copy.14 = f32[1,256,1024]{2,1,0:T(8,128)} copy(f32[1,256,1024]{2,1,0:T(8,128)} %get-tuple-element.8) | data formatting | bytes 2097152
  168.5 1.7 copy.15
  170.2 1.2 copy.16
  171.4 1.7 copy.17

commit v2 on v1

--- a/solution.py
+++ b/solution.py
@@ -34,6 +34,12 @@
     return lax.dot_general(a, b, dims, preferred_element_type=F32)
 
 
+def place(rz, c):
+    rz = rz % 8
+    near = 0 if rz == 0 else 2 * rz - 1 if rz <= 4 else 2 * (8 - rz)
+    return 2 * near + c
+
+
 def stack_heads(x):
     return jnp.concatenate([x[:, i * HD : (i + 1) * HD] for i in range(x.shape[1] // HD)], axis=0)
 
@@ -46,9 +52,9 @@
     hid, tea, seg, wq, wkv, gain,
     o_gq, o_gkv, o_gg, o_lig,
     w, hbuf, g16, acc, qkv, probs, mask, invb, outb, dyb,
-    usend, uall, dqall, msend, mrecv, bsend, asend, abuf, bbuf, bfin, lig, gtot, ggsend, ggrecv,
+    usend, uall, qown, qs, dqkv, dqall, msend, mrecv, bsend, asend, abuf, bbuf, bfin, lig, gtot, xsend, xrecv, ggsend, ggrecv,
     w_sem, g_ssem, g_rsem, h_ssem, h_rsem, u_ssem, u_rsem, q_ssem, q_rsem,
-    m_ssem, m_rsem, ab_ssem, a_rsem, b_rsem, f_rsem, l_ssem, l_rsem, gg_ssem, gg_rsem,
+    m_ssem, m_rsem, ab_ssem, a_rsem, b_rsem, f_rsem, l_ssem, l_rsem, gg_ssem, gg_rsem, x_ssem, x_rsem,
 ):
     s = lax.axis_index("section")
     d = lax.axis_index("dp")
@@ -75,14 +81,12 @@
         return 0
 
     lax.fori_loop(1, DP, greet, 0)
-    gt = d // 4
-    src_d = 4 * t + d // 4
-    quarter = lax.rem(d, 4)
-    loop = (gt == t) & (quarter == gt)
-    for tt in range(TENSOR):
-        @pl.when(jnp.logical_not(loop & (tt == t)))
+    loop = (t == z // 2) & (z // 4 == lax.rem(z, 2))
+    zs = 2 * t + d // 8
+    for i in range(8):
+        @pl.when(jnp.logical_not(loop & (t == i // 2) & (xl == i % 2)))
         def _():
-            pl.semaphore_signal(bar, inc=1, device_id=(s, src_d, tt), device_id_type=MESH)
+            pl.semaphore_signal(bar, inc=1, device_id=(s, 2 * zs + i % 2, i // 2), device_id_type=MESH)
 
     def w_copies(j):
         rows = pl.ds(pl.multiple_of(j * BLK, BLK), BLK)
@@ -104,7 +108,7 @@
     for i in range(4):
         g16[4 * t + i] = jnp.broadcast_to(gain[:, i * ROWS : (i + 1) * ROWS].astype(F32), (8, ROWS))
 
-    pl.semaphore_wait(bar, 26 - jnp.where(loop, 1, 0))
+    pl.semaphore_wait(bar, 30 - jnp.where(loop, 1, 0))
 
     def g_copy(i, dev_t):
         sl = g16.at[pl.ds(4 * t, 4)]
@@ -202,67 +206,94 @@
                     hn.astype(F32) - tea[0, m, :, k * HB : (k + 1) * HB].astype(F32)
                 ).astype(BF)
 
-    def u_copy(m, i):
-        p = lax.rem(d + i, DP)
-        return rcopy(usend.at[m, p], uall.at[m, d], u_ssem.at[m, i], u_rsem.at[m, d], (s, p, t))
+    def peer(rz, c):
+        return (s, 2 * lax.rem(z + rz % 8, 8) + (1 - xl if c else xl), t)
+
+    def u_copy(m, rz):
+        slot = place(-rz, 0) if rz else place(0, 1)
+        src = usend.at[m, lax.rem(z + rz, 8) if rz else z]
+        return rcopy(src, uall.at[m, slot], u_ssem.at[m, slot], u_rsem.at[m, slot], peer(rz, 0 if rz else 1))
+
+    def u_pass_copy(m, rz):
+        slot = place(rz, 1)
+        return rcopy(
+            uall.at[m, place(rz, 0)], uall.at[m, slot], u_ssem.at[m, slot], u_rsem.at[m, slot], peer(0, 1)
+        )
+
+    def u_pass(m):
+        for rz in (1, 7, 2, 6, 3, 5, 4):
+            u_wait_one(m, place(rz, 0))
+            u_pass_copy(m, rz).start()
+
+    def u_wait_one(m, i):
+        blk = uall.at[m, i]
+        rcopy(blk, blk, u_ssem.at[m, i], u_rsem.at[m, i], peer(1, 0)).wait_recv()
 
     def send_rows(m):
         inv = invb[m, :, 0:1]
         for j in range(TENSOR):
             for k in range(2):
                 u = (hbuf[m, j, k].astype(F32) * inv).astype(BF)
-                usend[m, 4 * j + 2 * k] = u[:, :ROWS]
-                usend[m, 4 * j + 2 * k + 1] = u[:, ROWS:]
-        uall[m, d] = usend[m, d]
-
-        def one(i, _):
-            u_copy(m, i).start()
-            return 0
-
-        lax.fori_loop(1, DP, one, 0)
-
-    def q_copy(m, src_d, sem, dev_d):
-        blk = dqall.at[m, src_d]
-        return rcopy(blk, blk, q_ssem.at[m, sem], q_rsem.at[m, src_d], (s, dev_d, t))
-
-    dx = d + 1 - 2 * xl
-    zr = lax.rem(z + 1, 8)
-    zl = lax.rem(z + 7, 8)
+                for i in range(4):
+                    usend[m, 2 * j + k, i] = u[:, i * HD : (i + 1) * HD]
+        for p in range(8):
+            usend[m, p, 4] = qkv[m, :, QC : QC + HD]
+        uall[m, 0] = usend[m, z]
+        for rz in (0, 1, 7, 2, 6, 3, 5, 4):
+            u_copy(m, rz).start()
+
+
+    def q_copy(m, src, rz, c, step, dc):
+        dst = place(rz - step, c ^ dc)
+        return rcopy(src, qs.at[m, dst], q_ssem.at[m, dst], q_rsem.at[m, dst], peer(step, dc))
+
+    def q_wait(m, rz, c):
+        blk = qs.at[m, place(rz, c)]
+        rcopy(blk, blk, q_ssem.at[m, 0], q_rsem.at[m, place(rz, c)], peer(1, 0)).wait_recv()
 
     def q_start(m):
-        q_copy(m, d, 0, dx).start()
-        q_copy(m, d, 1, 2 * zr + xl).start()
-        q_copy(m, d, 2, 2 * zl + xl).start()
-
-    def q_wait(m, src_d):
-        q_copy(m, src_d, 0, dx).wait_recv()
-
-    def q_hop(m, r, col):
-        cx = xl if col == 0 else 1 - xl
-        right = 2 * lax.rem(z + 8 - r, 8) + cx
-        left = 2 * lax.rem(z + r, 8) + cx
-        sem = 1 + 4 * r + 2 * col
-        if r > 0 or col == 1:
-            q_wait(m, right)
-            if r > 0:
-                q_wait(m, left)
-            if r < 3 or col == 0:
-                q_copy(m, right, sem, 2 * zr + xl).start()
-            if r < 3 or col == 1:
-                q_copy(m, left, sem + 1, 2 * zl + xl).start()
-
-    def q_finish(m):
-        for col in range(2):
-            q_wait(m, 2 * lax.rem(z + 4, 8) + (xl if col == 0 else 1 - xl))
+        qs[m, 0] = qown[m, xl]
+        for step in (2, 6, 1, 7, 0):
+            for c in range(2):
+                if step or c:
+                    q_copy(m, qown.at[m, 1 - xl if c else xl], 0, 0, step, c).start()
+
+    def q_hop(m):
+        for c in range(2):
+            for sg in (1, -1):
+                q_wait(m, -2 * sg, c)
+                src = qs.at[m, place(-2 * sg, c)]
+                q_copy(m, src, -2 * sg, c, sg, 0).start()
+                if c == (0 if sg == 1 else 1):
+                    q_copy(m, src, -2 * sg, c, 2 * sg, 0).start()
+
+    def q_near(m):
+        for rz, c in ((0, 1), (1, 0), (-1, 0), (1, 1), (-1, 1)):
+            q_wait(m, rz, c)
+
+    def q_far(m):
+        for rz in (3, -3, 4):
+            for c in range(2):
+                q_wait(m, rz, c)
+
+    def q_make(m, lo, hi):
+        for i in range(lo, hi):
+            keys = uall[m, i, 4]
+            none = jnp.zeros_like(keys)
+            pair = jnp.concatenate(
+                [jnp.concatenate([keys, none], axis=1), jnp.concatenate([none, keys], axis=1)], axis=0
+            )
+            dq = (dot(qs[m, i, : 2 * L, :], pair) * SCALE).astype(BF)
+            for h in range(4):
+                dqall[m, i, :, h * HD : (h + 1) * HD] = dq[
+                    (h % 2) * L : (h % 2 + 1) * L, (h // 2) * HD : (h // 2 + 1) * HD
+                ]
+            dqall[m, i, :, HB:] = qs[m, i, 2 * L :, :]
 
     def q_drain(m):
-        q_copy(m, d, 0, dx).wait_send()
-        for r in range(4):
-            for col in range(2):
-                if r < 3 or col == 0:
-                    q_copy(m, d, 1 + 4 * r + 2 * col, dx).wait_send()
-                if r < 3 or col == 1:
-                    q_copy(m, d, 2 + 4 * r + 2 * col, dx).wait_send()
+        for i in range(1, DP):
+            blk = qs.at[m, i]
+            rcopy(blk, blk, q_ssem.at[m, i], q_rsem.at[m, i], peer(1, 0)).wait_send()
 
     def m_copy(m, i, k):
         return rcopy(msend.at[m, i, k], mrecv.at[m, i, k], m_ssem.at[m, i, k], m_rsem.at[m, i, k], (s, d, t1))
@@ -278,6 +309,11 @@
 
     def l_copy(m, k):
         return rcopy(dyb.at[m, k], lig.at[m, k], l_ssem.at[m, k], l_rsem.at[m, k], (sn, d, t))
+
+    def early_hop():
+        @pl.when(s == 0)
+        def _():
+            q_hop(0)
 
     def backward(m):
         key = qkv[m, :, QC : QC + HD]
@@ -300,7 +336,9 @@
             dp = dot(do, val, NT)
             ds = (pr * (dp - jnp.sum(dp * pr, axis=1, keepdims=True))).astype(BF)
             dq = (dot(ds, key) * SCALE).astype(BF)
-            dqall[m, d, :, k * HB : (k + 1) * HB] = unstack_heads(dq)
+            dqkv[m, :, k * HB : (k + 1) * HB] = unstack_heads(dq)
+            qown[m, k, : 2 * L, :L] = ds[: 2 * L]
+            qown[m, k, : 2 * L, L:] = ds[2 * L :]
             dk += dot(ds, q, TN)
             dv += dot(pr.astype(BF), do, TN)
             qd = jnp.sum(q.astype(F32) * dq.astype(F32), axis=1, keepdims=True)
@@ -308,14 +346,18 @@
                 rd += qd[i * L : (i + 1) * L]
         dkb = (dk * SCALE).astype(BF)
         dvb = dv.astype(BF)
-        dqall[m, d, :, QC : QC + HD] = dkb
-        dqall[m, d, :, QC + HD :] = dvb
+        dqkv[m, :, QC : QC + HD] = dkb
+        dqkv[m, :, QC + HD :] = dvb
+        qown[m, 0, 2 * L :, :] = dkb
+        qown[m, 1, 2 * L :, :] = dvb
         rd += jnp.sum(
             key.astype(F32) * dkb.astype(F32) + val.astype(F32) * dvb.astype(F32), axis=1, keepdims=True
         )
         q_start(m)
+        if m == 1:
+            early_hop()
         coef = inv * inv * rd / D
-        grads = dqall[m, d]
+        grads = dqkv[m]
 
         def term(j, k):
             part = dot(grads, w[pl.ds(pl.multiple_of(j * BLK + k * HB, HB), HB), :], NT)
@@ -349,15 +391,60 @@
 
     for m in range(MB):
         forward(m)
-    for m in range(MB):
-        send_rows(m)
-    for m in range(MB):
-        backward(m)
-
-    for r in range(4):
+
+    @pl.when(s < SECTIONS - 1)
+    def _():
         for m in range(MB):
-            for col in range(2):
-                q_hop(m, r, col)
+            send_rows(m)
+
+    @pl.when(s < 2)
+    def _():
+        for m in range(MB):
+            u_pass(m)
+
+    backward(0)
+    backward(1)
+
+    @pl.when(s == SECTIONS - 1)
+    def _():
+        for m in range(MB):
+            send_rows(m)
+
+    @pl.when(s > 0)
+    def _():
+        q_hop(0)
+
+    @pl.when(s >= 2)
+    def _():
+        for m in range(MB):
+            u_pass(m)
+
+    def u_wait(m):
+        for rz in range(8):
+            u_wait_one(m, place(rz, 1))
+
+    def weight_grads(m, lo, hi, block, i):
+        u = uall[m, lo:hi, 2 * block + i].reshape((hi - lo) * L, HD)
+        g = dqall[m, lo:hi].reshape((hi - lo) * L, HB + HD)
+        part = dot(u, g, TN)
+        if m == 0 and lo == 0:
+            gtot[block, i] = part
+        else:
+            gtot[block, i] += part
+
+    u_wait(0)
+    q_near(0)
+    q_make(0, 0, 10)
+    q_hop(1)
+    u_wait(1)
+    q_far(0)
+    q_make(0, 10, DP)
+    q_near(1)
+    q_make(1, 0, 10)
+    for block in range(2):
+        for i in range(2):
+            weight_grads(0, 0, DP, block, i)
+            weight_grads(1, 0, 10, block, i)
 
     @pl.when(s == 0)
     def _():
@@ -376,53 +463,74 @@
         for k in range(2):
             o_lig[0, 0, m, :, k * HB : (k + 1) * HB] = lig[m, k]
 
-    for m in range(MB):
-        def u_wait(i, _):
-            p = lax.rem(d + i, DP)
-            rcopy(usend.at[m, p], uall.at[m, p], u_ssem.at[m, i], u_rsem.at[m, p], (s, p, t)).wait_recv()
-            return 0
-
-        lax.fori_loop(1, DP, u_wait, 0)
-        q_finish(m)
-        u = uall[m].reshape(DP * L, ROWS)
-        g = dqall[m].reshape(DP * L, C)
-        if m == 0:
-            gtot[...] = dot(u, g, TN)
-        else:
-            gtot[...] += dot(u, g, TN)
-
-    eye = lax.broadcasted_iota(jnp.int32, (ROWS, ROWS), 0) == lax.broadcasted_iota(jnp.int32, (ROWS, ROWS), 1)
-    total = gtot[...]
-    rows = pl.ds(pl.multiple_of(d * ROWS, ROWS), ROWS)
-    col = jnp.sum(total * w[rows, :].astype(F32), axis=1, keepdims=True)
-    row = jnp.sum(jnp.where(eye, jnp.broadcast_to(col, (ROWS, ROWS)), 0.0), axis=0, keepdims=True)
-    ggsend[...] = jnp.broadcast_to(row, (8, ROWS))
-
-    def gg_copy(j):
-        return rcopy(ggsend, ggrecv.at[t], gg_ssem.at[j], gg_rsem.at[t], (s, 4 * quarter + j, gt))
-
-    for j in range(4):
-        mine = loop & (quarter == j)
-
-        @pl.when(jnp.logical_not(mine))
+    q_far(1)
+    q_make(1, 10, DP)
+
+    def x_copy(i):
+        return rcopy(xsend.at[i], xrecv.at[i], x_ssem.at[i], x_rsem.at[i], peer(0, 1))
+
+    for i in range(2):
+        weight_grads(1, 10, DP, 1 - xl, i)
+        xsend[i] = gtot[1 - xl, i].astype(BF)
+        x_copy(i).start()
+    for i in range(2):
+        weight_grads(1, 10, DP, xl, i)
+
+    eye = lax.broadcasted_iota(jnp.int32, (HD, HD), 0) == lax.broadcasted_iota(jnp.int32, (HD, HD), 1)
+    for block in range(2):
+        for i in range(2):
+            rows = pl.ds(pl.multiple_of((2 * z + block) * ROWS + i * HD, HD), HD)
+            wide = w[rows, pl.ds(pl.multiple_of(xl * HB, HB), HB)].astype(F32)
+            narrow = w[rows, pl.ds(pl.multiple_of(QC + xl * HD, HD), HD)].astype(F32)
+            total = gtot[block, i]
+            col = jnp.sum(total[:, :HB] * wide, axis=1, keepdims=True) + jnp.sum(
+                total[:, HB:] * narrow, axis=1, keepdims=True
+            )
+            row = jnp.sum(jnp.where(eye, jnp.broadcast_to(col, (HD, HD)), 0.0), axis=0, keepdims=True)
+            ggsend[block, :, i * HD : (i + 1) * HD] = jnp.broadcast_to(row, (8, HD))
+
+    def gg_copy(block, j):
+        n = 4 * block + j
+        src = 2 * t + xl
+        return rcopy(
+            ggsend.at[block], ggrecv.at[src], gg_ssem.at[n], gg_rsem.at[src], (s, 8 * lax.rem(z, 2) + n, z // 2)
+        )
+
+    for block in range(2):
+        for j in range(4):
+            mine = loop & (lax.rem(d, 8) == 4 * block + j)
+
+            @pl.when(jnp.logical_not(mine))
+            def _():
+                gg_copy(block, j).start()
+
+            @pl.when(mine)
+            def _():
+                ggrecv[2 * t + xl] = ggsend[block]
+
+    for i in range(2):
+        x_copy(i).wait_recv()
+        grow = g16[d, 0:1, i * HD : (i + 1) * HD]
+        gcol = jnp.sum(jnp.where(eye, jnp.broadcast_to(grow, (HD, HD)), 0.0), axis=1, keepdims=True)
+        own = gtot[xl, i]
+        other = xrecv[i].astype(F32)
+        first = jnp.where(xl == 0, own, other) * gcol
+        second = jnp.where(xl == 0, other, own) * gcol
+        rs = slice(i * HD, (i + 1) * HD)
+        o_gq[0, rs, :HB] = first[:, :HB]
+        o_gq[0, rs, HB:] = second[:, :HB]
+        o_gkv[0, rs, :HD] = first[:, HB:]
+        o_gkv[0, rs, HD:] = second[:, HB:]
+
+    gsum = jnp.zeros((8, ROWS), F32)
+    for i in range(8):
+        @pl.when(jnp.logical_not(loop & (t == i // 2) & (xl == i % 2)))
         def _():
-            gg_copy(j).start()
-
-        @pl.when(mine)
-        def _():
-            ggrecv[t] = ggsend[...]
-
-    gcol = jnp.sum(
-        jnp.where(eye, jnp.broadcast_to(g16[d, 0:1, :], (ROWS, ROWS)), 0.0), axis=1, keepdims=True
-    )
-    o_gq[0] = total[:, :QC] * gcol
-    o_gkv[0] = total[:, QC:] * gcol
-
-    for tt in range(TENSOR):
-        @pl.when(jnp.logical_not(loop & (tt == t)))
-        def _():
-            rcopy(ggsend, ggrecv.at[tt], gg_ssem.at[0], gg_rsem.at[tt], (s, src_d, tt)).wait_recv()
-    gsum = ggrecv[0] + ggrecv[1] + ggrecv[2] + ggrecv[3]
+            rcopy(
+                ggsend.at[0], ggrecv.at[i], gg_ssem.at[0], gg_rsem.at[i], (s, 2 * zs + i % 2, i // 2)
+            ).wait_recv()
+        gsum += ggrecv[i]
+    quarter = lax.rem(d, 4)
     picked = jnp.zeros((1, L), F32)
     for j in range(4):
         picked += jnp.where(quarter == j, 1.0, 0.0) * gsum[0:1, j * L : (j + 1) * L]
@@ -453,18 +561,23 @@
             def _():
                 a_copy(m, k).wait_send()
 
-        def u_drain(i, _):
-            u_copy(m, i).wait_send()
-            return 0
-
-        lax.fori_loop(1, DP, u_drain, 0)
+        for rz in range(8):
+            u_copy(m, rz).wait_send()
+            if rz:
+                u_pass_copy(m, rz).wait_send()
         q_drain(m)
-    for j in range(4):
-        mine = loop & (quarter == j)
-
-        @pl.when(jnp.logical_not(mine))
-        def _():
-            gg_copy(j).wait_send()
+    for i in range(2):
+        x_copy(i).wait_send()
+    for block in range(2):
+        for j in range(4):
+            @pl.when(jnp.logical_not(loop & (lax.rem(d, 8) == 4 * block + j)))
+            def _():
+                gg_copy(block, j).wait_send()
+
+
+def hand_out(*refs):
+    for i in range(4):
+        refs[4 + i][...] = refs[i][...]
 
 
 def body(hidden_in, teacher, segment_ids, w_query, w_keyval, norm_gain):
@@ -493,9 +606,12 @@
             V((MB, L, 128), F32),
             V((MB, 2, L, HB), BF),
             V((MB, 2, L, HB), BF),
-            V((MB, DP, L, ROWS), BF),
-            V((MB, DP, L, ROWS), BF),
-            V((MB, DP, L, C), BF),
+            V((MB, 8, 5, L, HD), BF),
+            V((MB, DP, 5, L, HD), BF),
+            V((MB, 2, 3 * L, HD), BF),
+            V((MB, DP, 3 * L, HD), BF),
+            V((MB, L, C), BF),
+            V((MB, DP, L, HB + HD), BF),
             V((MB, 2, 2, L, HB), BF),
             V((MB, 2, 2, L, HB), BF),
             V((MB, 2, L, HB), BF),
@@ -504,9 +620,11 @@
             V((MB, 2, L, HB), BF),
             V((MB, 2, L, HB), BF),
             V((MB, 2, L, HB), BF),
-            V((ROWS, C), F32),
-            V((8, ROWS), F32),
-            V((TENSOR, 8, ROWS), F32),
+            V((2, 2, HD, HB + HD), F32),
+            V((2, HD, HB + HD), BF),
+            V((2, HD, HB + HD), BF),
+            V((2, 8, ROWS), F32),
+            V((8, 8, ROWS), F32),
             dma((2, TENSOR)),
             dma((3,)),
             dma((TENSOR,)),
@@ -514,7 +632,7 @@
             dma((MB, TENSOR, 2)),
             dma((MB, DP)),
             dma((MB, DP)),
-            dma((MB, 17)),
+            dma((MB, DP)),
             dma((MB, DP)),
             dma((MB, 2, 2)),
             dma((MB, 2, 2)),
@@ -524,15 +642,23 @@
             dma((MB, 2)),
             dma((MB, 2)),
             dma((MB, 2)),
-            dma((4,)),
-            dma((TENSOR,)),
+            dma((8,)),
+            dma((8,)),
+            dma((2,)),
+            dma((2,)),
         ],
         compiler_params=pltpu.CompilerParams(
             collective_id=1, has_side_effects=True, vmem_limit_bytes=58 * 1024 * 1024
         ),
         name="train_step",
     )(hidden_in, teacher, segment_ids, w_query, w_keyval, norm_gain)
-    return out
+    return pl.pallas_call(
+        hand_out,
+        out_shape=tuple(jax.ShapeDtypeStruct(o.shape, o.dtype) for o in out),
+        in_specs=[vmem] * 4,
+        out_specs=(vmem,) * 4,
+        name="hand_out",
+    )(*out)
 
 
 def solution(mesh):

time: 176 us -> 146 us (0.83); the launches traced: 173 us -> 146 us
  Pallas kernels: 166 us -> 145 us
  local copies, waits for them, and re-layouts: 6.83 us -> 0 us
    pallas_call x1, Pallas kernels: 166 us -> 143 us  [body(): pl.pallas_call(kernel, out_shape=(jax.ShapeDtypeStruct((1, ROWS, QC), F32...]
    unnamed x4 -> x0, local copies, waits for them, and re-layouts: 6.83 us -> none
    pallas_call x0 -> x1, Pallas kernels: none -> 2.51 us  [body(): pl.pallas_call(hand_out, out_shape=tuple((jax.ShapeDtypeStruct(o.shape, o...]
where the time goes in v2:
time: 146 us
  Pallas kernels  145 us (99%)
    pallas_call x1, Pallas kernels, body(): pl.pallas_call(kernel, out_shape=(jax.ShapeDtypeStruct((1, ROWS, QC), F32...  143 us

profile of v2, /device:TPU:2, one launch (start us, length us, event | category | flops | bytes accessed | tf_op | source)
XLA Modules:
  0.0 145.7 jit_solution(14109129079244352155)
XLA Ops:
  0.6 142.6 %train_step.1 = (f32[1,256,1024]{2,1,0:T(8,128)}, f32[1,256,256]{2,1,0:T(8,128)}, f32[1,64]{1,0:T(1,128)}, bf16[1,1,2,64,1024]{4,3,2,1,0:T(8,128)(2,1)}) custom-call(bf16[1,2,64,1024]{3,2,1,0:T(8,128)(2,1)} %hid.1, bf16[1,2,64,1024]{3,2,1,0:T(8,128)(2,1)} %tea.1, s32[1,2,64]{2,1,0:T(2,128)} %seg.1, bf16[1,4096,1024]{2,1,0:T(8,128)(2,1)} %wq.1, ...), custom_call_target="tpu_custom_call" | custom-call | tf_op jit(solution)/shard_map/train_step/pallas_call | solution.py:588
  143.2 2.5 %hand_out.1 = (f32[1,256,1024]{2,1,0:T(8,128)}, f32[1,256,256]{2,1,0:T(8,128)}, f32[1,64]{1,0:T(1,128)}, bf16[1,1,2,64,1024]{4,3,2,1,0:T(8,128)(2,1)}) custom-call(f32[1,256,1024]{2,1,0:T(8,128)} %get-tuple-element.8.refs_0_, f32[1,256,256]{2,1,0:T(8,128)} %get-tuple-element.9.refs_1_, f32[1,64]{1,0:T(1,128)} %get-tuple-element.10.refs_2_, ...), custom_call_target="tpu_custom_call" | custom-call | tf_op jit(solution)/shard_map/hand_out/pallas_call | solution.py:655

commit v3 on v2

--- a/solution.py
+++ b/solution.py
@@ -11,6 +11,7 @@
 D = 4096
 HD = 128
 L = 64
+W = 32
 MB = 2
 DP = 16
 SECTIONS = 4
@@ -52,7 +53,7 @@
     hid, tea, seg, wq, wkv, gain,
     o_gq, o_gkv, o_gg, o_lig,
     w, hbuf, g16, acc, qkv, probs, mask, invb, outb, dyb,
-    usend, uall, qown, qs, dqkv, dqall, msend, mrecv, bsend, asend, abuf, bbuf, bfin, lig, gtot, xsend, xrecv, ggsend, ggrecv,
+    usend, uall, qown, qs, low, kdiag, dqkv, dqall, msend, mrecv, bsend, asend, abuf, bbuf, bfin, lig, gtot, xsend, xrecv, ggsend, ggrecv,
     w_sem, g_ssem, g_rsem, h_ssem, h_rsem, u_ssem, u_rsem, q_ssem, q_rsem,
     m_ssem, m_rsem, ab_ssem, a_rsem, b_rsem, f_rsem, l_ssem, l_rsem, gg_ssem, gg_rsem, x_ssem, x_rsem,
 ):
@@ -95,7 +96,7 @@
             pltpu.make_async_copy(wkv.at[0, rows, :], w.at[rows, pl.ds(QC, KC)], w_sem.at[1, j]),
         )
 
-    for j in (t, t1, t2, t3):
+    for j in (t, t2, t1, t3):
         for c in w_copies(j):
             c.start()
 
@@ -105,6 +106,11 @@
         srow = jnp.broadcast_to(seg[0, m : m + 1, :], (L, L))
         scol = jnp.sum(jnp.where(ri == ci, srow, 0), axis=1, keepdims=True)
         mask[m] = jnp.where((srow == scol) & (ri >= ci), 1.0, 0.0)
+    fi = lax.broadcasted_iota(jnp.int32, (L, HD), 0)
+    fj = lax.rem(lax.broadcasted_iota(jnp.int32, (L, HD), 1), W)
+    low[0] = jnp.where(fj > fi - W, 1.0, 0.0).astype(BF)
+    low[1] = jnp.where(fj > fi - W, 0.0, 1.0).astype(BF)
+    kdiag[...] = jnp.zeros_like(kdiag)
     for i in range(4):
         g16[4 * t + i] = jnp.broadcast_to(gain[:, i * ROWS : (i + 1) * ROWS].astype(F32), (8, ROWS))
 
@@ -157,28 +163,32 @@
                 for c in w_copies(j):
                     c.wait()
 
-        for k in range(2):
+        def arrive(k):
             @pl.when(s > 0)
             def _():
                 h_wait(m, t, k)
             h_copy(m, k, 2, t, hbuf.at[m, t, k], (s, d, t1)).start()
-        need_w(t)
-        for k in range(2):
-            ss += kstep(t, k, k == 0)
-        for k in range(2):
             h_wait(m, t2, k)
             h_copy(m, k, 3, t2, hbuf.at[m, t2, k], (s, d, t1)).start()
+
+        arrive(0)
+        need_w(t)
+        ss += kstep(t, 0, True)
+        need_w(t2)
+        ss += kstep(t2, 0, False)
+        arrive(1)
         need_w(t1)
-        for k in range(2):
-            h_wait(m, t1, k)
-            ss += kstep(t1, k, False)
-        need_w(t2)
-        for k in range(2):
-            ss += kstep(t2, k, False)
+        h_wait(m, t1, 0)
+        ss += kstep(t1, 0, False)
         need_w(t3)
-        for k in range(2):
-            h_wait(m, t3, k)
-            ss += kstep(t3, k, False)
+        h_wait(m, t3, 0)
+        ss += kstep(t3, 0, False)
+        ss += kstep(t, 1, False)
+        ss += kstep(t2, 1, False)
+        h_wait(m, t1, 1)
+        ss += kstep(t1, 1, False)
+        h_wait(m, t3, 1)
+        ss += kstep(t3, 1, False)
         inv = lax.rsqrt(ss / D + EPSILON)
         invb[m] = jnp.broadcast_to(inv, (L, 128))
         qkv[m] = (acc[...] * inv).astype(BF)
@@ -278,17 +288,14 @@
 
     def q_make(m, lo, hi):
         for i in range(lo, hi):
-            keys = uall[m, i, 4]
-            none = jnp.zeros_like(keys)
-            pair = jnp.concatenate(
-                [jnp.concatenate([keys, none], axis=1), jnp.concatenate([none, keys], axis=1)], axis=0
-            )
-            dq = (dot(qs[m, i, : 2 * L, :], pair) * SCALE).astype(BF)
+            pair = kdiag.at[i % 2]
             for h in range(4):
-                dqall[m, i, :, h * HD : (h + 1) * HD] = dq[
-                    (h % 2) * L : (h % 2 + 1) * L, (h // 2) * HD : (h // 2 + 1) * HD
-                ]
-            dqall[m, i, :, HB:] = qs[m, i, 2 * L :, :]
+                pair[h * W : (h + 1) * W, h * HD : (h + 1) * HD] = uall[m, i, 4, :W]
+                pair[HD + h * W : HD + (h + 1) * W, h * HD : (h + 1) * HD] = uall[m, i, 4, W:]
+            fold = qs[m, i, :L, :]
+            both = jnp.concatenate([fold * low[0], fold * low[1]], axis=1)
+            dqall[m, i, :, :HB] = (dot(both, pair[...]) * SCALE).astype(BF)
+            dqall[m, i, :, HB:] = qs[m, i, L:, :]
 
     def q_drain(m):
         for i in range(1, DP):
@@ -334,12 +341,14 @@
             q = stack_heads(qkv[m, :, k * HB : (k + 1) * HB])
             pr = probs[m, k]
             dp = dot(do, val, NT)
-            ds = (pr * (dp - jnp.sum(dp * pr, axis=1, keepdims=True))).astype(BF)
-            dq = (dot(ds, key) * SCALE).astype(BF)
+            ds = pr * (dp - jnp.sum(dp * pr, axis=1, keepdims=True))
+            dsb = ds.astype(BF)
+            dq = (dot(dsb, key) * SCALE).astype(BF)
             dqkv[m, :, k * HB : (k + 1) * HB] = unstack_heads(dq)
-            qown[m, k, : 2 * L, :L] = ds[: 2 * L]
-            qown[m, k, : 2 * L, L:] = ds[2 * L :]
-            dk += dot(ds, q, TN)
+            fold = (ds[:, :W] + ds[:, W:]).astype(BF)
+            for h in range(4):
+                qown[m, k, :L, h * W : (h + 1) * W] = fold[h * L : (h + 1) * L]
+            dk += dot(dsb, q, TN)
             dv += dot(pr.astype(BF), do, TN)
             qd = jnp.sum(q.astype(F32) * dq.astype(F32), axis=1, keepdims=True)
             for i in range(4):
@@ -348,8 +357,8 @@
         dvb = dv.astype(BF)
         dqkv[m, :, QC : QC + HD] = dkb
         dqkv[m, :, QC + HD :] = dvb
-        qown[m, 0, 2 * L :, :] = dkb
-        qown[m, 1, 2 * L :, :] = dvb
+        qown[m, 0, L:, :] = dkb
+        qown[m, 1, L:, :] = dvb
         rd += jnp.sum(
             key.astype(F32) * dkb.astype(F32) + val.astype(F32) * dvb.astype(F32), axis=1, keepdims=True
         )
@@ -363,8 +372,8 @@
             part = dot(grads, w[pl.ds(pl.multiple_of(j * BLK + k * HB, HB), HB), :], NT)
             return inv * gains(j, k) * part - hbuf[m, j, k].astype(F32) * coef
 
-        for i, j in enumerate((t3, t1)):
-            for k in range(2):
+        for k in range(2):
+            for i, j in enumerate((t3, t1)):
                 msend[m, i, k] = term(j, k).astype(BF)
                 m_copy(m, i, k).start()
         for k in range(2):
@@ -380,7 +389,6 @@
             def _():
                 f_copy(m, k).start()
 
-        for k in range(2):
             own = term(t, k) + dyb[m, k].astype(F32)
             m_copy(m, 1, k).wait_recv()
             asend[m, k] = (own + mrecv[m, 1, k].astype(F32)).astype(BF)
@@ -608,8 +616,10 @@
             V((MB, 2, L, HB), BF),
             V((MB, 8, 5, L, HD), BF),
             V((MB, DP, 5, L, HD), BF),
-            V((MB, 2, 3 * L, HD), BF),
-            V((MB, DP, 3 * L, HD), BF),
+            V((MB, 2, 2 * L, HD), BF),
+            V((MB, DP, 2 * L, HD), BF),
+            V((2, L, HD), BF),
+            V((2, 2 * HD, HB), BF),
             V((MB, L, C), BF),
             V((MB, DP, L, HB + HD), BF),
             V((MB, 2, 2, L, HB), BF),

time: 146 us -> 136 us (0.932)
  Pallas kernels: 145 us -> 136 us
    pallas_call x1, Pallas kernels: 143 us -> 133 us  [body(): pl.pallas_call(kernel, out_shape=(jax.ShapeDtypeStruct((1, ROWS, QC), F32...]
where the time goes in v3:
time: 136 us
  Pallas kernels  136 us (100%)
    pallas_call x1, Pallas kernels, body(): pl.pallas_call(kernel, out_shape=(jax.ShapeDtypeStruct((1, ROWS, QC), F32...  133 us

profile of v3, /device:TPU:2, one launch (start us, length us, event | category | flops | bytes accessed | tf_op | source)
XLA Modules:
  0.0 136.3 jit_solution(12816217809849657757)
XLA Ops:
  0.6 133.2 %train_step.1 = (f32[1,256,1024]{2,1,0:T(8,128)}, f32[1,256,256]{2,1,0:T(8,128)}, f32[1,64]{1,0:T(1,128)}, bf16[1,1,2,64,1024]{4,3,2,1,0:T(8,128)(2,1)}) custom-call(bf16[1,2,64,1024]{3,2,1,0:T(8,128)(2,1)} %hid.1, bf16[1,2,64,1024]{3,2,1,0:T(8,128)(2,1)} %tea.1, s32[1,2,64]{2,1,0:T(2,128)} %seg.1, bf16[1,4096,1024]{2,1,0:T(8,128)(2,1)} %wq.1, ...), custom_call_target="tpu_custom_call" | custom-call | tf_op jit(solution)/shard_map/train_step/pallas_call | solution.py:596
  133.8 2.5 %hand_out.1 = (f32[1,256,1024]{2,1,0:T(8,128)}, f32[1,256,256]{2,1,0:T(8,128)}, f32[1,64]{1,0:T(1,128)}, bf16[1,1,2,64,1024]{4,3,2,1,0:T(8,128)(2,1)}) custom-call(f32[1,256,1024]{2,1,0:T(8,128)} %get-tuple-element.8.refs_0_, f32[1,256,256]{2,1,0:T(8,128)} %get-tuple-element.9.refs_1_, f32[1,64]{1,0:T(1,128)} %get-tuple-element.10.refs_2_, ...), custom_call_target="tpu_custom_call" | custom-call | tf_op jit(solution)/shard_map/hand_out/pallas_call | solution.py:665

commit v4 on v3

--- a/solution.py
+++ b/solution.py
@@ -52,9 +52,9 @@
 def kernel(
     hid, tea, seg, wq, wkv, gain,
     o_gq, o_gkv, o_gg, o_lig,
-    w, hbuf, g16, acc, qkv, probs, mask, invb, outb, dyb,
+    w, hbuf, g16, acc, qkv, probs, mask, invb, pown, pbuf, dyb,
     usend, uall, qown, qs, low, kdiag, dqkv, dqall, msend, mrecv, bsend, asend, abuf, bbuf, bfin, lig, gtot, xsend, xrecv, ggsend, ggrecv,
-    w_sem, g_ssem, g_rsem, h_ssem, h_rsem, u_ssem, u_rsem, q_ssem, q_rsem,
+    w_sem, g_ssem, g_rsem, h_ssem, h_rsem, p_ssem, p_rsem, u_ssem, u_rsem, q_ssem, q_rsem,
     m_ssem, m_rsem, ab_ssem, a_rsem, b_rsem, f_rsem, l_ssem, l_rsem, gg_ssem, gg_rsem, x_ssem, x_rsem,
 ):
     s = lax.axis_index("section")
@@ -120,18 +120,34 @@
         sl = g16.at[pl.ds(4 * t, 4)]
         return rcopy(sl, sl, g_ssem.at[i], g_rsem.at[t], (s, d, dev_t))
 
-    def h_copy(m, k, kind, slot, src, dev):
-        return rcopy(src, hbuf.at[m, slot, k], h_ssem.at[m, kind, k], h_rsem.at[m, slot, k], dev)
+    def hid_copy(m, k, kind):
+        slot = t2 if kind == 2 else t
+        src = hbuf.at[m, slot, k] if kind == 2 else hid.at[0, m, :, pl.ds(k * HB, HB)]
+        return rcopy(
+            src, hbuf.at[m, slot, k], h_ssem.at[m, kind, k], h_rsem.at[m, slot, k], (s, d, t1 if kind else t2)
+        )
+
+    def h_wait(m, slot, k):
+        blk = hbuf.at[m, slot, k]
+        rcopy(blk, blk, h_ssem.at[m, 0, k], h_rsem.at[m, slot, k], (s, d, t1)).wait_recv()
+
+    def p_copy(m, src, layer, slot, kind):
+        dev = ((sn, d, t), (sn, d, t2), (s, d, t1), (s, d, t1))[kind]
+        return rcopy(
+            src, pbuf.at[m, layer, slot], p_ssem.at[m, layer, kind], p_rsem.at[m, layer, slot], dev
+        )
+
+    def p_wait(m, layer, slot):
+        p_copy(m, pbuf.at[m, layer, slot], layer, slot, 2).wait_recv()
 
     for i, tt in enumerate((t1, t2, t3)):
         g_copy(i, tt).start()
 
-    @pl.when(s == 0)
-    def _():
-        for m in range(MB):
-            for k in range(2):
-                hbuf[m, t, k] = hid[0, m, :, k * HB : (k + 1) * HB]
-                h_copy(m, k, 4, t, hbuf.at[m, t, k], (s, d, t2)).start()
+    for m in range(MB):
+        for k in range(2):
+            hid_copy(m, k, 0).start()
+            hid_copy(m, k, 1).start()
+            hbuf[m, t, k] = hid[0, m, :, k * HB : (k + 1) * HB]
 
     for tt in (t1, t2, t3):
         sl = g16.at[pl.ds(4 * tt, 4)]
@@ -140,9 +156,6 @@
     def gains(j, k):
         p = 4 * j + 2 * k
         return jnp.concatenate([g16[p, 0:1, :], g16[p + 1, 0:1, :]], axis=1)
-
-    def h_wait(m, slot, k):
-        h_copy(m, k, 0, slot, hbuf.at[m, slot, k], (s, d, t1)).wait_recv()
 
     def forward(m):
         ss = jnp.zeros((L, 1), F32)
@@ -163,32 +176,64 @@
                 for c in w_copies(j):
                     c.wait()
 
-        def arrive(k):
-            @pl.when(s > 0)
-            def _():
-                h_wait(m, t, k)
-            h_copy(m, k, 2, t, hbuf.at[m, t, k], (s, d, t1)).start()
+        def rebuild(layer, j, b):
+            vd = kdiag.at[b]
+            for h in range(4):
+                vd[h * W : (h + 1) * W, h * HD : (h + 1) * HD] = pbuf[m, layer, j, 2, :W]
+                vd[HD + h * W : HD + (h + 1) * W, h * HD : (h + 1) * HD] = pbuf[m, layer, j, 2, W:]
+            for k in range(2):
+                fold = pbuf[m, layer, j, k]
+                both = jnp.concatenate([fold * low[0], fold * low[1]], axis=1)
+                o = dot(both, vd[...]).astype(BF)
+                hbuf[m, j, k] = (hbuf[m, j, k].astype(F32) + o.astype(F32)).astype(BF)
+
+        for k in range(2):
             h_wait(m, t2, k)
-            h_copy(m, k, 3, t2, hbuf.at[m, t2, k], (s, d, t1)).start()
-
-        arrive(0)
+            hid_copy(m, k, 2).start()
+
+        @pl.when(s > 0)
+        def _():
+            for k in range(2):
+                hid_copy(m, k, 2).wait_send()
+
+        for layer in range(SECTIONS - 1):
+            @pl.when(s > layer)
+            def _():
+                mine = pbuf.at[m, layer, t]
+                p_wait(m, layer, t)
+                p_copy(m, mine, layer, t, 2).start()
+
+                @pl.when(s < SECTIONS - 1)
+                def _():
+                    p_copy(m, mine, layer, t, 1).start()
+                    p_copy(m, mine, layer, t, 0).start()
+
+                p_wait(m, layer, t2)
+                p_copy(m, pbuf.at[m, layer, t2], layer, t2, 3).start()
+                rebuild(layer, t, 0)
+                rebuild(layer, t2, 1)
+
         need_w(t)
         ss += kstep(t, 0, True)
+        ss += kstep(t, 1, False)
         need_w(t2)
         ss += kstep(t2, 0, False)
-        arrive(1)
-        need_w(t1)
-        h_wait(m, t1, 0)
-        ss += kstep(t1, 0, False)
-        need_w(t3)
-        h_wait(m, t3, 0)
-        ss += kstep(t3, 0, False)
-        ss += kstep(t, 1, False)
         ss += kstep(t2, 1, False)
-        h_wait(m, t1, 1)
-        ss += kstep(t1, 1, False)
-        h_wait(m, t3, 1)
-        ss += kstep(t3, 1, False)
+        for j in (t1, t3):
+            for k in range(2):
+                h_wait(m, j, k)
+        for layer in range(SECTIONS - 1):
+            @pl.when(s > layer)
+            def _():
+                p_wait(m, layer, t1)
+                rebuild(layer, t1, 0)
+                p_wait(m, layer, t3)
+                rebuild(layer, t3, 1)
+
+        for j in (t1, t3):
+            need_w(j)
+            ss += kstep(j, 0, False)
+            ss += kstep(j, 1, False)
         inv = lax.rsqrt(ss / D + EPSILON)
         invb[m] = jnp.broadcast_to(inv, (L, 128))
         qkv[m] = (acc[...] * inv).astype(BF)
@@ -201,20 +246,24 @@
             e = jnp.exp(jnp.where(allowed, sc, -1e30))
             pr = e / jnp.sum(e, axis=1, keepdims=True)
             probs[m, k] = pr
-            o = dot(pr.astype(BF), val).astype(BF)
-            hn = (hbuf[m, t, k].astype(F32) + unstack_heads(o).astype(F32)).astype(BF)
-            outb[m, k] = hn
-
-            @pl.when(s < SECTIONS - 1)
-            def _():
-                h_copy(m, k, 0, t, outb.at[m, k], (sn, d, t)).start()
-                h_copy(m, k, 1, t, outb.at[m, k], (sn, d, t2)).start()
+            fold = (pr[:, :W] + pr[:, W:]).astype(BF)
+            for h in range(4):
+                pown[m, k, :, h * W : (h + 1) * W] = fold[h * L : (h + 1) * L]
 
             @pl.when(s == SECTIONS - 1)
             def _():
+                o = unstack_heads(dot(pr.astype(BF), val).astype(BF)).astype(F32)
+                hn = (hbuf[m, t, k].astype(F32) + o).astype(BF)
                 dyb[m, k] = (
                     hn.astype(F32) - tea[0, m, :, k * HB : (k + 1) * HB].astype(F32)
                 ).astype(BF)
+
+        pown[m, 2] = val
+
+        @pl.when(s < SECTIONS - 1)
+        def _():
+            p_copy(m, pown.at[m], s, t, 1).start()
+            p_copy(m, pown.at[m], s, t, 0).start()
 
     def peer(rz, c):
         return (s, 2 * lax.rem(z + rz % 8, 8) + (1 - xl if c else xl), t)
@@ -548,17 +597,15 @@
         g_copy(i, tt).wait_send()
     for m in range(MB):
         for k in range(2):
-            h_copy(m, k, 2, t, hbuf.at[m, t, k], (s, d, t1)).wait_send()
-            h_copy(m, k, 3, t2, hbuf.at[m, t2, k], (s, d, t1)).wait_send()
+            hid_copy(m, k, 0).wait_send()
+            hid_copy(m, k, 1).wait_send()
 
             @pl.when(s == 0)
             def _():
-                h_copy(m, k, 4, t, hbuf.at[m, t, k], (s, d, t2)).wait_send()
+                hid_copy(m, k, 2).wait_send()
 
             @pl.when(s < SECTIONS - 1)
             def _():
-                h_copy(m, k, 0, t, outb.at[m, k], (sn, d, t)).wait_send()
-                h_copy(m, k, 1, t, outb.at[m, k], (sn, d, t2)).wait_send()
                 l_copy(m, k).wait_send()
 
             for i in range(2):
@@ -568,6 +615,17 @@
             @pl.when(s > 0)
             def _():
                 a_copy(m, k).wait_send()
+
+        for layer in range(SECTIONS - 1):
+            @pl.when((s < SECTIONS - 1) & (s >= layer))
+            def _():
+                p_copy(m, pown.at[m], layer, t, 0).wait_send()
+                p_copy(m, pown.at[m], layer, t, 1).wait_send()
+
+            @pl.when(s > layer)
+            def _():
+                p_copy(m, pown.at[m], layer, t, 2).wait_send()
+                p_copy(m, pown.at[m], layer, t2, 3).wait_send()
 
         for rz in range(8):
             u_copy(m, rz).wait_send()
@@ -612,7 +670,8 @@
             V((MB, 2, 4 * L, L), F32),
             V((MB, L, L), F32),
             V((MB, L, 128), F32),
-            V((MB, 2, L, HB), BF),
+            V((MB, 3, L, HD), BF),
+            V((MB, SECTIONS - 1, TENSOR, 3, L, HD), BF),
             V((MB, 2, L, HB), BF),
             V((MB, 8, 5, L, HD), BF),
             V((MB, DP, 5, L, HD), BF),
@@ -638,8 +697,10 @@
             dma((2, TENSOR)),
             dma((3,)),
             dma((TENSOR,)),
-            dma((MB, 5, 2)),
+            dma((MB, 3, 2)),
             dma((MB, TENSOR, 2)),
+            dma((MB, SECTIONS - 1, 4)),
+            dma((MB, SECTIONS - 1, TENSOR)),
             dma((MB, DP)),
             dma((MB, DP)),
             dma((MB, DP)),

time: 136 us -> 130 us (0.956)
  Pallas kernels: 136 us -> 129 us
    pallas_call x1, Pallas kernels: 133 us -> 127 us  [body(): pl.pallas_call(kernel, out_shape=(jax.ShapeDtypeStruct((1, ROWS, QC), F32...]
where the time goes in v4:
time: 130 us
  Pallas kernels  129 us (99%)
    pallas_call x1, Pallas kernels, body(): pl.pallas_call(kernel, out_shape=(jax.ShapeDtypeStruct((1, ROWS, QC), F32...  127 us

profile of v4, /device:TPU:2, one launch (start us, length us, event | category | flops | bytes accessed | tf_op | source)
XLA Modules:
  0.0 130.1 jit_solution(18039910051895727886)
XLA Ops:
  0.6 126.9 %train_step.1 = (f32[1,256,1024]{2,1,0:T(8,128)}, f32[1,256,256]{2,1,0:T(8,128)}, f32[1,64]{1,0:T(1,128)}, bf16[1,1,2,64,1024]{4,3,2,1,0:T(8,128)(2,1)}) custom-call(bf16[1,2,64,1024]{3,2,1,0:T(8,128)(2,1)} %hid.1, bf16[1,2,64,1024]{3,2,1,0:T(8,128)(2,1)} %tea.1, s32[1,2,64]{2,1,0:T(2,128)} %seg.1, bf16[1,4096,1024]{2,1,0:T(8,128)(2,1)} %wq.1, ...), custom_call_target="tpu_custom_call" | custom-call | tf_op jit(solution)/shard_map/train_step/pallas_call | solution.py:654
  127.6 2.5 %hand_out.1 = (f32[1,256,1024]{2,1,0:T(8,128)}, f32[1,256,256]{2,1,0:T(8,128)}, f32[1,64]{1,0:T(1,128)}, bf16[1,1,2,64,1024]{4,3,2,1,0:T(8,128)(2,1)}) custom-call(f32[1,256,1024]{2,1,0:T(8,128)} %get-tuple-element.8.refs_0_, f32[1,256,256]{2,1,0:T(8,128)} %get-tuple-element.9.refs_1_, f32[1,64]{1,0:T(1,128)} %get-tuple-element.10.refs_2_, ...), custom_call_target="tpu_custom_call" | custom-call | tf_op jit(solution)/shard_map/hand_out/pallas_call | solution.py:726

commit v5 on v4

--- a/solution.py
+++ b/solution.py
@@ -52,9 +52,9 @@
 def kernel(
     hid, tea, seg, wq, wkv, gain,
     o_gq, o_gkv, o_gg, o_lig,
-    w, hbuf, g16, acc, qkv, probs, mask, invb, pown, pbuf, dyb,
+    w, hidv, teav, hbuf, g16, acc, qkv, probs, mask, invb, pown, pbuf, dyb,
     usend, uall, qown, qs, low, kdiag, dqkv, dqall, msend, mrecv, bsend, asend, abuf, bbuf, bfin, lig, gtot, xsend, xrecv, ggsend, ggrecv,
-    w_sem, g_ssem, g_rsem, h_ssem, h_rsem, p_ssem, p_rsem, u_ssem, u_rsem, q_ssem, q_rsem,
+    w_sem, in_sem, g_ssem, g_rsem, h_ssem, h_rsem, p_ssem, p_rsem, u_ssem, u_rsem, q_ssem, q_rsem,
     m_ssem, m_rsem, ab_ssem, a_rsem, b_rsem, f_rsem, l_ssem, l_rsem, gg_ssem, gg_rsem, x_ssem, x_rsem,
 ):
     s = lax.axis_index("section")
@@ -96,6 +96,14 @@
             pltpu.make_async_copy(wkv.at[0, rows, :], w.at[rows, pl.ds(QC, KC)], w_sem.at[1, j]),
         )
 
+    def in_copy(i, m, k):
+        src = (hid, tea)[i].at[0, m, :, pl.ds(k * HB, HB)]
+        return pltpu.make_async_copy(src, (hidv, teav)[i].at[m, k], in_sem.at[i, m, k])
+
+    for i in range(2):
+        for m in range(MB):
+            for k in range(2):
+                in_copy(i, m, k).start()
     for j in (t, t2, t1, t3):
         for c in w_copies(j):
             c.start()
@@ -114,6 +122,9 @@
     for i in range(4):
         g16[4 * t + i] = jnp.broadcast_to(gain[:, i * ROWS : (i + 1) * ROWS].astype(F32), (8, ROWS))
 
+    for m in range(MB):
+        for k in range(2):
+            in_copy(0, m, k).wait()
     pl.semaphore_wait(bar, 30 - jnp.where(loop, 1, 0))
 
     def g_copy(i, dev_t):
@@ -122,7 +133,7 @@
 
     def hid_copy(m, k, kind):
         slot = t2 if kind == 2 else t
-        src = hbuf.at[m, slot, k] if kind == 2 else hid.at[0, m, :, pl.ds(k * HB, HB)]
+        src = hbuf.at[m, slot, k] if kind == 2 else hidv.at[m, k]
         return rcopy(
             src, hbuf.at[m, slot, k], h_ssem.at[m, kind, k], h_rsem.at[m, slot, k], (s, d, t1 if kind else t2)
         )
@@ -147,7 +158,8 @@
         for k in range(2):
             hid_copy(m, k, 0).start()
             hid_copy(m, k, 1).start()
-            hbuf[m, t, k] = hid[0, m, :, k * HB : (k + 1) * HB]
+            hbuf[m, t, k] = hidv[m, k]
+            in_copy(1, m, k).wait()
 
     for tt in (t1, t2, t3):
         sl = g16.at[pl.ds(4 * tt, 4)]
@@ -160,16 +172,16 @@
     def forward(m):
         ss = jnp.zeros((L, 1), F32)
 
-        def kstep(j, k, first):
-            x = hbuf[m, j, k].astype(F32)
-            part_ss = jnp.sum(x * x, axis=1, keepdims=True)
-            xg = (x * gains(j, k)).astype(BF)
-            part = dot(xg, w[pl.ds(pl.multiple_of(j * BLK + k * HB, HB), HB), :])
+        def kstep(j, first):
+            x0 = hbuf[m, j, 0].astype(F32)
+            x1 = hbuf[m, j, 1].astype(F32)
+            xg = jnp.concatenate([(x0 * gains(j, 0)).astype(BF), (x1 * gains(j, 1)).astype(BF)], axis=1)
+            part = dot(xg, w[pl.ds(pl.multiple_of(j * BLK, BLK), BLK), :])
             if first:
                 acc[...] = part
             else:
                 acc[...] += part
-            return part_ss
+            return jnp.sum(x0 * x0 + x1 * x1, axis=1, keepdims=True)
 
         def need_w(j):
             if m == 0:
@@ -214,11 +226,9 @@
                 rebuild(layer, t2, 1)
 
         need_w(t)
-        ss += kstep(t, 0, True)
-        ss += kstep(t, 1, False)
+        ss += kstep(t, True)
         need_w(t2)
-        ss += kstep(t2, 0, False)
-        ss += kstep(t2, 1, False)
+        ss += kstep(t2, False)
         for j in (t1, t3):
             for k in range(2):
                 h_wait(m, j, k)
@@ -232,8 +242,7 @@
 
         for j in (t1, t3):
             need_w(j)
-            ss += kstep(j, 0, False)
-            ss += kstep(j, 1, False)
+            ss += kstep(j, False)
         inv = lax.rsqrt(ss / D + EPSILON)
         invb[m] = jnp.broadcast_to(inv, (L, 128))
         qkv[m] = (acc[...] * inv).astype(BF)
@@ -255,7 +264,7 @@
                 o = unstack_heads(dot(pr.astype(BF), val).astype(BF)).astype(F32)
                 hn = (hbuf[m, t, k].astype(F32) + o).astype(BF)
                 dyb[m, k] = (
-                    hn.astype(F32) - tea[0, m, :, k * HB : (k + 1) * HB].astype(F32)
+                    hn.astype(F32) - teav[m, k].astype(F32)
                 ).astype(BF)
 
         pown[m, 2] = val
@@ -446,8 +455,14 @@
             def _():
                 a_copy(m, k).start()
 
-    for m in range(MB):
-        forward(m)
+    forward(0)
+
+    @pl.when(s == SECTIONS - 1)
+    def _():
+        backward(0)
+        send_rows(0)
+
+    forward(1)
 
     @pl.when(s < SECTIONS - 1)
     def _():
@@ -459,13 +474,15 @@
         for m in range(MB):
             u_pass(m)
 
-    backward(0)
+    @pl.when(s < SECTIONS - 1)
+    def _():
+        backward(0)
+
     backward(1)
 
     @pl.when(s == SECTIONS - 1)
     def _():
-        for m in range(MB):
-            send_rows(m)
+        send_rows(1)
 
     @pl.when(s > 0)
     def _():
@@ -642,8 +659,22 @@
 
 
 def hand_out(*refs):
-    for i in range(4):
-        refs[4 + i][...] = refs[i][...]
+    src, dst, held = refs[:4], refs[4:8], refs[8:12]
+    isem, osem = refs[12:]
+    parts = [(0, slice(i * L, (i + 1) * L)) for i in range(4)] + [(1, None), (3, None), (2, None)]
+
+    def at(ref, part):
+        return ref if part is None else ref.at[:, part]
+
+    ins = [pltpu.make_async_copy(at(src[i], q), at(held[i], q), isem.at[n]) for n, (i, q) in enumerate(parts)]
+    outs = [pltpu.make_async_copy(at(held[i], q), at(dst[i], q), osem.at[n]) for n, (i, q) in enumerate(parts)]
+    for c in ins:
+        c.start()
+    for i, o in zip(ins, outs):
+        i.wait()
+        o.start()
+    for o in outs:
+        o.wait()
 
 
 def body(hidden_in, teacher, segment_ids, w_query, w_keyval, norm_gain):
@@ -659,10 +690,12 @@
             jax.ShapeDtypeStruct((1, L), F32),
             jax.ShapeDtypeStruct((1, 1, MB, L, BLK), BF),
         ),
-        in_specs=[vmem, vmem, vmem, hbm, hbm, vmem],
+        in_specs=[hbm, hbm, vmem, hbm, hbm, vmem],
         out_specs=(vmem, vmem, vmem, vmem),
         scratch_shapes=[
             V((D, C), BF),
+            V((MB, 2, L, HB), BF),
+            V((MB, 2, L, HB), BF),
             V((MB, TENSOR, 2, L, HB), BF),
             V((DP, 8, ROWS), F32),
             V((L, C), F32),
@@ -695,6 +728,7 @@
             V((2, 8, ROWS), F32),
             V((8, 8, ROWS), F32),
             dma((2, TENSOR)),
+            dma((2, MB, 2)),
             dma((3,)),
             dma((TENSOR,)),
             dma((MB, 3, 2)),
@@ -726,8 +760,9 @@
     return pl.pallas_call(
         hand_out,
         out_shape=tuple(jax.ShapeDtypeStruct(o.shape, o.dtype) for o in out),
-        in_specs=[vmem] * 4,
-        out_specs=(vmem,) * 4,
+        in_specs=[hbm] * 4,
+        out_specs=(hbm,) * 4,
+        scratch_shapes=[V(o.shape, o.dtype) for o in out] + [dma((7,)), dma((7,))],
         name="hand_out",
     )(*out)
 

time: 130 us -> 128 us (0.985)
  the two profiles are of different devices: /device:TPU:2 before, /device:TPU:16 now
where the time goes in v5:
time: 128 us
  Pallas kernels  127 us (99%)
    pallas_call x1, Pallas kernels, body(): pl.pallas_call(kernel, out_shape=(jax.ShapeDtypeStruct((1, ROWS, QC), F32...  125 us

profile of v5, /device:TPU:16, one launch (start us, length us, event | category | flops | bytes accessed | tf_op | source)
XLA Modules:
  0.0 127.7 jit_solution(12134550138995540605)
XLA Ops:
  0.6 124.7 %train_step.1 = (f32[1,256,1024]{2,1,0:T(8,128)}, f32[1,256,256]{2,1,0:T(8,128)}, f32[1,64]{1,0:T(1,128)}, bf16[1,1,2,64,1024]{4,3,2,1,0:T(8,128)(2,1)}) custom-call(bf16[1,2,64,1024]{3,2,1,0:T(8,128)(2,1)} %hid.1, bf16[1,2,64,1024]{3,2,1,0:T(8,128)(2,1)} %tea.1, s32[1,2,64]{2,1,0:T(2,128)} %seg.1, bf16[1,4096,1024]{2,1,0:T(8,128)(2,1)} %wq.1, ...), custom_call_target="tpu_custom_call" | custom-call | tf_op jit(solution)/shard_map/train_step/pallas_call | solution.py:685
  125.4 2.2 %hand_out.1 = (f32[1,256,1024]{2,1,0:T(8,128)}, f32[1,256,256]{2,1,0:T(8,128)}, f32[1,64]{1,0:T(1,128)}, bf16[1,1,2,64,1024]{4,3,2,1,0:T(8,128)(2,1)}) custom-call(f32[1,256,1024]{2,1,0:T(8,128)} %get-tuple-element.8.refs_0_, f32[1,256,256]{2,1,0:T(8,128)} %get-tuple-element.9.refs_1_, f32[1,64]{1,0:T(1,128)} %get-tuple-element.10.refs_2_, ...), custom_call_target="tpu_custom_call" | custom-call | tf_op jit(solution)/shard_map/hand_out/pallas_call | solution.py:760

commit v6 on v5

--- a/solution.py
+++ b/solution.py
@@ -478,6 +478,10 @@
     def _():
         backward(0)
 
+    @pl.when(s == 2)
+    def _():
+        u_pass(0)
+
     backward(1)
 
     @pl.when(s == SECTIONS - 1)
@@ -488,10 +492,13 @@
     def _():
         q_hop(0)
 
+    @pl.when(s == 3)
+    def _():
+        u_pass(0)
+
     @pl.when(s >= 2)
     def _():
-        for m in range(MB):
-            u_pass(m)
+        u_pass(1)
 
     def u_wait(m):
         for rz in range(8):

time: 128 us -> 132 us (1.031)
  the two profiles are of different devices: /device:TPU:16 before, /device:TPU:2 now
where the time goes in v6:
time: 132 us; the launch traced here: 131 us
  Pallas kernels  131 us (99%)
    pallas_call x1, Pallas kernels, body(): pl.pallas_call(kernel, out_shape=(jax.ShapeDtypeStruct((1, ROWS, QC), F32...  128 us

profile of v6, /device:TPU:2, one launch (start us, length us, event | category | flops | bytes accessed | tf_op | source)
XLA Modules:
  0.0 131.4 jit_solution(12556106376273931861)
XLA Ops:
  0.6 128.4 %train_step.1 = (f32[1,256,1024]{2,1,0:T(8,128)}, f32[1,256,256]{2,1,0:T(8,128)}, f32[1,64]{1,0:T(1,128)}, bf16[1,1,2,64,1024]{4,3,2,1,0:T(8,128)(2,1)}) custom-call(bf16[1,2,64,1024]{3,2,1,0:T(8,128)(2,1)} %hid.1, bf16[1,2,64,1024]{3,2,1,0:T(8,128)(2,1)} %tea.1, s32[1,2,64]{2,1,0:T(2,128)} %seg.1, bf16[1,4096,1024]{2,1,0:T(8,128)(2,1)} %wq.1, ...), custom_call_target="tpu_custom_call" | custom-call | tf_op jit(solution)/shard_map/train_step/pallas_call | solution.py:692
  129.0 2.2 %hand_out.1 = (f32[1,256,1024]{2,1,0:T(8,128)}, f32[1,256,256]{2,1,0:T(8,128)}, f32[1,64]{1,0:T(1,128)}, bf16[1,1,2,64,1024]{4,3,2,1,0:T(8,128)(2,1)}) custom-call(f32[1,256,1024]{2,1,0:T(8,128)} %get-tuple-element.8.refs_0_, f32[1,256,256]{2,1,0:T(8,128)} %get-tuple-element.9.refs_1_, f32[1,64]{1,0:T(1,128)} %get-tuple-element.10.refs_2_, ...), custom_call_target="tpu_custom_call" | custom-call | tf_op jit(solution)/shard_map/hand_out/pallas_call | solution.py:767
